TPU v7x, 32 devices: a whole 2x2x4 slice. The times are simulated.
32 devices in a mesh: img: 16 (over z, y, x), grp: 2 (over core).
Axes of the slice: x: 2, y: 2, z: 4, core: 2. Of those that a mesh axis runs over, the one named last changes fastest.
Arguments:
- tokens: bfloat16 [512, 8, 1024], P('img'), may hold values from -16 to 16
- w_embed: bfloat16 [1024, 768], replicated, may hold values from -0.1875 to 0.1875
- w_query: bfloat16 [768, 768], replicated, may hold values from -1 to 1
- w_key: bfloat16 [768, 768], replicated, may hold values from -1 to 1
- w_value: bfloat16 [768, 768], replicated, may hold values from -0.21875 to 0.21875
- w_out: bfloat16 [768, 768], replicated, may hold values from -0.21875 to 0.21875
- w_head: bfloat16 [768, 28], replicated, may hold values from -0.109375 to 0.109375
- pair_images: int32 [16, 2, 64, 2], replicated, may hold values from 0 to 511, as said below
- pair_counts: int32 [16, 2], replicated, may hold values from 48 to 64, as said below
- owner_row: int32 [512], replicated, may hold values from 0 to 511, as said below
Outputs:
- joined_geometry: float32 [512, 32], P('img')
- joined_descriptors: float32 [512, 192], P('img')
Inputs may be any that keep to these rules, and one draw needn't show every extreme that they name: `pair_images`: the owner of an image is owner_row of it integer-divided by 32. Among the 256 views of the pair slots of one chip (both cores, live or not), no owner holds more than 16; in every draw some owner holds exactly 16 live ones of some chip. The two images of a pair have different owners. `pair_counts`: slots at or beyond the count are ignored; some executor has 64. `owner_row`: A permutation.
All inputs are finite; a program needn't handle non-finite values.
Results may differ from a plain program's by a relative error of at most 0.0065.
Values may be sent and summed in bfloat16 or wider, within the bound.
A program may use at most 64 MiB of HBM per device.

v0:
```python
import math

import jax
import jax.numpy as jnp
from jax import lax
from jax.sharding import PartitionSpec as P

HEADS = 12
PAIR_BLOCK = 8


def layer_norm(values):
    center = values - jnp.mean(values, axis=-1, keepdims=True)
    spread = jnp.mean(center * center, axis=-1, keepdims=True)
    return center * lax.rsqrt(spread + 1e-05)


def contribution(head_out):
    confidence = 1.0 + jnp.exp(head_out[..., 3:4, :])
    return jnp.concatenate(
        [confidence * head_out[..., :3, :], confidence, confidence * head_out[..., 4:, :]], axis=-2
    )


def join(totals, patches, channels):
    image_count = totals.shape[0]
    shaped = totals.reshape(image_count, channels, patches)
    confidence = shaped[:, 3:4, :]
    geometry = jnp.concatenate(
        [shaped[:, :3, :] / (1.0 + confidence), jnp.log1p(confidence)], axis=1
    )
    descriptors = shaped[:, 4:, :] / (1.0 + confidence)
    return (
        geometry.reshape(image_count, 4 * patches),
        descriptors.reshape(image_count, (channels - 4) * patches),
    )


def decode_block(embedded, w_query, w_key, w_value, w_out, w_head):
    blocks, side_count, patches, dec_width = embedded.shape
    head_size = dec_width // HEADS
    normed = layer_norm(embedded.astype(jnp.float32)).astype(jnp.bfloat16)

    def project(weight):
        projected = jnp.einsum("bspd,de->bspe", normed, weight, preferred_element_type=jnp.float32)
        return projected.astype(jnp.bfloat16).reshape(blocks, side_count, patches, HEADS, head_size)

    queries = project(w_query)
    key_proj = project(w_key)[:, ::-1]
    value_proj = project(w_value)[:, ::-1]
    scores = jnp.einsum(
        "bsphd,bsqhd->bshpq", queries, key_proj, preferred_element_type=jnp.float32
    ) / math.sqrt(head_size)
    weights = jax.nn.softmax(scores, axis=-1).astype(jnp.bfloat16)
    attended = jnp.einsum(
        "bshpq,bsqhd->bsphd", weights, value_proj, preferred_element_type=jnp.float32
    )
    attended = attended.astype(jnp.bfloat16).reshape(blocks, side_count, patches, dec_width)
    mixed_rows = embedded.astype(jnp.float32) + jnp.einsum(
        "bspd,de->bspe", attended, w_out, preferred_element_type=jnp.float32
    )
    mixed_rows = mixed_rows.astype(jnp.bfloat16)
    head_out = jnp.einsum("bspd,dc->bscp", mixed_rows, w_head, preferred_element_type=jnp.float32)
    return contribution(head_out).reshape(blocks, side_count, -1)


def per_device(
    tokens, w_embed, w_query, w_key, w_value, w_out, w_head, pair_images, pair_counts, owner_row
):
    img_dev, patches, enc_width = tokens.shape
    channels = w_head.shape[1]
    owners = lax.axis_size("img")
    groups = lax.axis_size("grp")
    pair_cap = pair_images.shape[2]
    slot_cap = max(2, (2 * groups * pair_cap + owners - 1) // owners)
    my_chip = lax.axis_index("img")
    my_group = lax.axis_index("grp")
    end_count = groups * pair_cap * 2
    token_rows = owner_row[pair_images].reshape(owners, end_count)
    source_owner = token_rows // img_dev
    local_row = token_rows % img_dev
    end_index = jnp.arange(end_count, dtype=jnp.int32)
    earlier = end_index[None, :] < end_index[:, None]
    same_owner = source_owner[:, :, None] == source_owner[:, None, :]
    ranked = jnp.sum((same_owner & earlier[None]).astype(jnp.int32), axis=2)
    is_live = jnp.arange(pair_cap, dtype=jnp.int32)[None, None, :] < pair_counts[:, :, None]
    group_table = jnp.broadcast_to(jnp.arange(groups, dtype=jnp.int32)[:, None], (groups, pair_cap))
    slot_table = jnp.broadcast_to(
        jnp.arange(pair_cap, dtype=jnp.int32)[None, :], (groups, pair_cap)
    )
    dest_group = jnp.broadcast_to(group_table.reshape(1, -1), (owners, groups * pair_cap))
    dest_slot = jnp.broadcast_to(slot_table.reshape(1, -1), (owners, groups * pair_cap))
    my_share = pair_counts[my_chip, my_group]
    live_end = jnp.repeat(is_live.reshape(owners, -1), 2, axis=1)
    group_end = jnp.repeat(dest_group, 2, axis=1)
    slot_end = jnp.repeat(dest_slot, 2, axis=1)
    side_end = end_index % 2
    to_send = live_end & (group_end == my_group) & (source_owner == my_chip)
    slot_index = jnp.arange(slot_cap, dtype=jnp.int32)
    matched = to_send[:, None, :] & (ranked[:, None, :] == slot_index[None, :, None])
    send_index = jnp.sum(jnp.where(matched, local_row[:, None, :], 0), axis=2)
    send_valid = jnp.any(matched, axis=2)
    mine = live_end[my_chip] & (group_end[my_chip] == my_group)
    pair_index = jnp.arange(pair_cap, dtype=jnp.int32)
    side_index = jnp.arange(2, dtype=jnp.int32)
    wanted = mine[None, None, :] & (slot_end[my_chip][None, None, :] == pair_index[:, None, None])
    wanted = wanted & (side_end[None, None, :] == side_index[None, :, None])
    flat_source = source_owner[my_chip] * slot_cap + ranked[my_chip]
    recv_index = jnp.sum(jnp.where(wanted, flat_source[None, None, :], 0), axis=2)
    recv_valid = jnp.any(wanted, axis=2)
    send_mask = send_valid[:, :, None, None].astype(jnp.bfloat16)
    embedded_own = jnp.dot(
        tokens.reshape(img_dev * patches, enc_width), w_embed, preferred_element_type=jnp.float32
    )
    embedded_own = embedded_own.astype(jnp.bfloat16).reshape(img_dev, patches, -1)
    outgoing = embedded_own[send_index] * send_mask
    received = lax.all_to_all(outgoing, "img", split_axis=0, concat_axis=0, tiled=True)
    pair_views = received.reshape(owners * slot_cap, patches, -1)[recv_index]

    def run_block(index_block, totals):
        first_row = index_block * PAIR_BLOCK
        block_views = lax.dynamic_slice_in_dim(pair_views, first_row, PAIR_BLOCK, 0)
        block_result = decode_block(block_views, w_query, w_key, w_value, w_out, w_head)
        return lax.dynamic_update_slice_in_dim(totals, block_result, first_row, 0)

    block_count = (my_share + PAIR_BLOCK - 1) // PAIR_BLOCK
    results = lax.fori_loop(
        0, block_count, run_block, jnp.zeros((pair_cap, 2, channels * patches), jnp.float32)
    )
    results = results * recv_valid[:, :, None].astype(jnp.float32)
    return_map = (
        jnp.arange(owners * slot_cap, dtype=jnp.int32)[:, None] == recv_index.reshape(1, -1)
    ) & recv_valid.reshape(1, -1)
    outgoing_back = jnp.dot(
        return_map.astype(jnp.float32),
        results.reshape(pair_cap * 2, -1),
        precision=lax.Precision.HIGHEST,
        preferred_element_type=jnp.float32,
    )
    returned = lax.all_to_all(
        outgoing_back.reshape(owners, slot_cap, -1), "img", split_axis=0, concat_axis=0, tiled=True
    )
    owner_map = (
        jnp.arange(img_dev, dtype=jnp.int32)[:, None] == send_index.reshape(1, -1)
    ) & send_valid.reshape(1, -1)
    owner_partial = jnp.dot(
        owner_map.astype(jnp.float32),
        returned.reshape(owners * slot_cap, -1),
        precision=lax.Precision.HIGHEST,
        preferred_element_type=jnp.float32,
    )
    totals = lax.psum(owner_partial, "grp")
    return join(totals, patches, channels)


def solution(mesh):
    in_specs = (P("img", None, None), P(), P(), P(), P(), P(), P(), P(), P(), P())
    out_specs = (P("img", None), P("img", None))
    return jax.shard_map(
        per_device, mesh=mesh, in_specs=in_specs, out_specs=out_specs, check_vma=False
    )
```

profile of v0, /device:TPU:0, one launch (start us, length us, event | category | flops | bytes accessed | tf_op | source)
XLA Modules:
  0.0 277.5 jit_solution(5922852846508975613)
XLA Ops:
  5.6 25.9 %gather_fusion = s32[4096]{0:T(1024)S(1)} fusion(s32[512]{0:T(512)S(1)} %copy-done.1, s32[4096]{0:T(1024)S(1)} %broadcast_clamp_fusion), kind=kCustom, calls=%fused_computation | custom fusion | bytes 49152 | tf_op jit(solution)/shard_map/gather | solution.py:79
  34.4 2.4 gather_fusion.1
  36.8 3.9 %broadcast_multiply_fusion.1 = bf16[16,16,8,768]{3,2,1,0:T(8,128)(2,1)} fusion(bf16[16,16,8,768]{3,2,1,0:T(8,128)(2,1)} %bitcast.109, bf16[16,16]{1,0:T(8,128)(2,1)S(1)} %convert_element_type.54), kind=kLoop, calls=%fused_computation.51 | loop fusion | flops 1572864 | bytes 6291968 | tf_op jit(solution)/shard_map/mul | solution.py:116
  40.7 8.5 %all-to-all-start = ((bf16[16,16,8,768]{3,2,1,0:T(8,128)(2,1)}), bf16[16,16,8,768]{3,2,1,0:T(8,128)(2,1)}, u32[]{:S(2)}, u32[]{:S(2)}) async-start(bf16[16,16,8,768]{3,2,1,0:T(8,128)(2,1)} %broadcast_multiply_fusion.1), calls=%async_computation | async-start | bytes 6291456 | tf_op jit(solution)/shard_map/all_to_all | solution.py:117
  52.1 58.2 %all-to-all-done = bf16[16,16,8,768]{3,2,1,0:T(8,128)(2,1)} async-done(((bf16[16,16,8,768]{3,2,1,0:T(8,128)(2,1)}), bf16[16,16,8,768]{3,2,1,0:T(8,128)(2,1)}, u32[]{:S(2)}, u32[]{:S(2)}) %all-to-all-start) | async-done | bytes 3145760 | tf_op jit(solution)/shard_map/all_to_all | solution.py:117
  110.2 3.7 %gather_fusion.2 = bf16[128,8,768]{2,1,0:T(8,128)(2,1)} fusion(bf16[256,8,768]{2,1,0:T(8,128)(2,1)} %bitcast.20, s32[1024]{0:T(1024)S(1)} %pad_clamp_fusion), kind=kCustom, calls=%fused_computation.2 | custom fusion | bytes 3146240 | tf_op jit(solution)/shard_map/gather | solution.py:118
  114.6 131.7 %while.10 = (s32[]{:T(128)}, f32[64,2,224]{2,0,1:T(8,128)}, s32[]{:T(128)}, bf16[64,2,8,768]{3,2,1,0:T(8,128)(2,1)}, bf16[768,768]{1,0:T(8,128)(2,1)}, /*index=5...) while((s32[]{:T(128)}, f32[64,2,224]{2,0,1:T(8,128)}, ...), condition=%wide.region_10.11_spmd, body=%wide.region_5.10_spmd.sunk | while | flops 616759424 | bytes 15685859 | solution.py:127
  116.8 1.7 fusion.120
  118.9 1.7 fusion.121
  122.7 1.7 fusion.119
  124.8 2.2 fusion.123
  128.5 1.4 fusion.124
  133.2 1.7 fusion.120
  135.4 1.7 fusion.121
  139.1 1.7 fusion.119
  141.3 2.2 fusion.123
  145.0 1.4 fusion.124
  149.7 1.7 fusion.120
  151.8 1.8 fusion.121
  155.6 1.7 fusion.119
  157.7 2.2 fusion.123
  161.5 1.4 fusion.124
  166.1 1.7 fusion.120
  168.3 1.8 fusion.121
  172.1 1.7 fusion.119
  174.2 2.2 fusion.123
  182.6 1.7 fusion.120
  184.7 1.7 fusion.121
  188.5 1.7 fusion.119
  190.7 2.2 fusion.123
  194.4 1.4 fusion.124
  199.1 1.7 fusion.120
  201.2 1.7 fusion.121
  205.0 1.7 fusion.119
  207.1 2.2 fusion.123
  215.6 1.7 fusion.120
  217.7 1.7 fusion.121
  221.5 1.7 fusion.119
  223.6 2.2 fusion.123
  227.3 1.4 fusion.124
  232.0 1.8 fusion.120
  234.2 1.7 fusion.121
  237.9 1.7 fusion.119
  240.1 2.2 fusion.123
  243.8 1.4 fusion.124
  248.5 15.0 %all-to-all-start.1 = ((f32[16,16,224]{2,1,0:T(8,128)}), f32[16,16,224]{2,1,0:T(8,128)S(1)}, u32[]{:S(2)}, u32[]{:S(2)}) async-start(f32[16,16,224]{2,1,0:T(8,128)} %fusion.56), calls=%async_computation.1 | async-start | bytes 524288 | tf_op jit(solution)/shard_map/all_to_all | solution.py:140
  263.7 8.3 %all-to-all-done.1 = f32[16,16,224]{2,1,0:T(8,128)S(1)} async-done(((f32[16,16,224]{2,1,0:T(8,128)}), f32[16,16,224]{2,1,0:T(8,128)S(1)}, u32[]{:S(2)}, u32[]{:S(2)}) %all-to-all-start.1) | async-done | bytes 229408 | tf_op jit(solution)/shard_map/all_to_all | solution.py:140
  272.4 3.7 %psum.7 = f32[32,28,8]{0,2,1:T(8,128)S(1)} all-reduce(f32[32,28,8]{0,2,1:T(8,128)S(1)} %convolution_bitcast_fusion), channel_id=1, replica_groups=mesh['img'=16,'grp'=2] {'grp'}, use_global_device_ids=true, to_apply=%region_11.12 | all-reduce | flops 7168 | bytes 57344 | tf_op jit(solution)/shard_map/psum | solution.py:152
  (271 shorter events, 77.0 us)
Async XLA Ops:
  0.6 33.1 %copy-start = (bf16[1024,768]{1,0:T(8,128)(2,1)S(1)}, bf16[1024,768]{1,0:T(8,128)(2,1)}, u32[]{:S(2)}) copy-start(bf16[1024,768]{1,0:T(8,128)(2,1)} %param.13) | copy-start | bytes 4718596
  0.6 4.9 %copy-start.1 = (s32[512]{0:T(512)S(1)}, s32[512]{0:T(512)}, u32[]{:S(2)}) copy-start(s32[512]{0:T(512)} %param.21) | copy-start | bytes 6148
  2.3 0.8 copy-start.10
  3.2 0.7 copy-start.4
  5.6 26.0 %copy-start.7 = (pred[16,256]{1,0:T(8,128)(4,1)S(1)}, pred[16,256]{1,0:T(8,128)(4,1)}, u32[]{:S(2)}) copy-start(pred[16,256]{1,0:T(8,128)(4,1)} %copy.136) | copy-start | bytes 12292
  5.6 26.0 %copy-start.9 = (pred[256]{0:T(512)(128)(4,1)S(1)}, pred[256]{0:T(512)(128)(4,1)}, u32[]{:S(2)}) copy-start(pred[256]{0:T(512)(128)(4,1)} %eq.144) | copy-start | bytes 772
  5.6 26.0 %copy-start.6 = (pred[256,256]{1,0:T(8,128)(4,1)S(1)}, pred[256,256]{1,0:T(8,128)(4,1)}, u32[]{:S(2)}) copy-start(pred[256,256]{1,0:T(8,128)(4,1)} %iota_compare_fusion.1) | copy-start | bytes 196612
  5.6 28.1 %copy-start.12 = (bf16[32,8,1024]{2,1,0:T(8,128)(2,1)S(1)}, bf16[32,8,1024]{2,1,0:T(8,128)(2,1)}, u32[]{:S(2)}) copy-start(bf16[32,8,1024]{2,1,0:T(8,128)(2,1)} %param.12) | copy-start | bytes 1572868
  40.7 8.5 %copy-start.8 = (s32[16,2]{0,1:T(2,128)S(1)}, s32[16,2]{0,1:T(2,128)}, u32[]{:S(2)}) copy-start(s32[16,2]{0,1:T(2,128)} %param.20) | copy-start | bytes 388
  40.7 9.8 %copy-start.5 = (pred[16,256]{0,1:T(8,128)(4,1)S(1)}, pred[16,256]{0,1:T(8,128)(4,1)}, u32[]{:S(2)}) copy-start(pred[16,256]{0,1:T(8,128)(4,1)} %copy-done.4) | copy-start | bytes 12292
  40.7 10.0 %copy-start.11 = (s32[128]{0:T(128)S(1)}, s32[128]{0:T(128)}, u32[]{:S(2)}) copy-start(s32[128]{0:T(128)} %copy-done.10) | copy-start | bytes 1540
  40.7 69.5 %all-to-all-start = ((bf16[16,16,8,768]{3,2,1,0:T(8,128)(2,1)}), bf16[16,16,8,768]{3,2,1,0:T(8,128)(2,1)}, u32[]{:S(2)}, u32[]{:S(2)}) async-start(bf16[16,16,8,768]{3,2,1,0:T(8,128)(2,1)} %broadcast_multiply_fusion.1), calls=%async_computation | async-start | bytes 6291456 | tf_op jit(solution)/shard_map/all_to_all | solution.py:117
  110.2 4.3 %copy-start.3 = (bf16[768,28]{0,1:T(8,128)(2,1)S(1)}, bf16[768,28]{0,1:T(8,128)(2,1)}, u32[]{:S(2)}) copy-start(bf16[768,28]{0,1:T(8,128)(2,1)} %param.18) | copy-start | bytes 129028
  127.0 1.5 copy-start.2
  143.5 1.5 copy-start.2
  159.9 1.5 copy-start.2
  176.4 1.5 copy-start.2
  192.9 1.5 copy-start.2
  209.3 1.5 copy-start.2
  225.8 1.5 copy-start.2
  242.3 1.5 copy-start.2
  248.5 23.5 %all-to-all-start.1 = ((f32[16,16,224]{2,1,0:T(8,128)}), f32[16,16,224]{2,1,0:T(8,128)S(1)}, u32[]{:S(2)}, u32[]{:S(2)}) async-start(f32[16,16,224]{2,1,0:T(8,128)} %fusion.56), calls=%async_computation.1 | async-start | bytes 524288 | tf_op jit(solution)/shard_map/all_to_all | solution.py:140
where the time goes:
time: 280 us; the launch traced here: 278 us
  matrix products  86.3 us (31%)
  local copies, waits for them, and re-layouts  67.2 us (24%)
  waiting for transfers between devices  66.5 us (24%)
  other arithmetic  27.4 us (10%)
  starting transfers between devices  23.5 us (8%)
  blocking collectives  3.69 us (1%)
    all_to_all x1, waiting for transfers between devices, per_device(): lax.all_to_all(outgoing, 'img', split_axis=0, concat_axis=0, tiled=True)  58.2 us
    dot_general x24, matrix products, project(): jnp.einsum('bspd,de->bspe', normed, weight, preferred_element_type=jnp.fl...  41.9 us
    gather x1, local copies, waits for them, and re-layouts, per_device(): token_rows = owner_row[pair_images].reshape(owners, end_count)  25.9 us
    dot_general x8, matrix products, decode_block(): jnp.einsum('bshpq,bsqhd->bsphd', weights, value_proj, preferred_element_t...  17.7 us
    all_to_all x1, starting transfers between devices, per_device(): lax.all_to_all(outgoing_back.reshape(owners, slot_cap, -1), 'img', split_...  15 us
    dot_general x8, matrix products, decode_block(): jnp.einsum('bspd,dc->bscp', mixed_rows, w_head, preferred_element_type=jn...  11.3 us
    sub x8, matrix products, decode_block(): weights = jax.nn.softmax(scores, axis=-1).astype(jnp.bfloat16)  10.6 us
    convert_element_type x8, local copies, waits for them, and re-layouts, decode_block(): attended.astype(jnp.bfloat16)  9.6 us
  transfers between devices with their start and end apart: 2, of which 2 were waited for; matrix products, arithmetic and copies ran while one was open for 1% of the time, Pallas kernels for 0%

commit v1 on v0

--- a/solution.py
+++ b/solution.py
@@ -1,12 +1,18 @@
+import functools
 import math
 
 import jax
 import jax.numpy as jnp
 from jax import lax
+from jax.experimental import pallas as pl
+from jax.experimental.pallas import tpu as pltpu
 from jax.sharding import PartitionSpec as P
 
 HEADS = 12
 PAIR_BLOCK = 8
+GATHER_LIMIT = 16 * 2**20
+TABLE = 128
+LANES = 128
 
 
 def layer_norm(values):
@@ -64,7 +70,7 @@
     return contribution(head_out).reshape(blocks, side_count, -1)
 
 
-def per_device(
+def by_executor(
     tokens, w_embed, w_query, w_key, w_value, w_out, w_head, pair_images, pair_counts, owner_row
 ):
     img_dev, patches, enc_width = tokens.shape
@@ -153,6 +159,219 @@
     return join(totals, patches, channels)
 
 
+def split3(values):
+    high = values.astype(jnp.bfloat16)
+    rest = values - high.astype(jnp.float32)
+    middle = rest.astype(jnp.bfloat16)
+    low = (rest - middle.astype(jnp.float32)).astype(jnp.bfloat16)
+    return jnp.concatenate([high, middle, low], axis=0)
+
+
+def sum3(values):
+    part = values.shape[0] // 3
+    return values[:part] + values[part : 2 * part] + values[2 * part :]
+
+
+NT = (((1,), (1,)), ((), ()))
+
+
+def decode_kernel(
+    heads, source_ref, local_ref, normed_ref, query_ref, key_ref, value_ref, base_ref, place_ref,
+    live_ref, out_ref, partner_rows, query_rows, attended
+):
+    ends = source_ref.shape[0]
+    patches, width = normed_ref.shape[1:]
+    channels = base_ref.shape[0]
+    head_size = width // heads
+    rows = ends * patches
+
+    def fetch(end, carry):
+        at = pl.ds(pl.multiple_of(end * patches, patches), patches)
+        own = pl.ds(pl.multiple_of(local_ref[end] * patches, patches), patches)
+        partner_rows[at, :] = normed_ref[source_ref[end]].astype(jnp.float32)
+        query_rows[at, :] = query_ref[own, :]
+        return carry
+
+    lax.fori_loop(0, ends, fetch, 0, unroll=8)
+
+    chunk = min(256, rows)
+    group = LANES
+    side = LANES // head_size
+    lane = lax.broadcasted_iota(jnp.int32, (group, LANES), 1)
+    column = lax.broadcasted_iota(jnp.int32, (patches, side * group), 1)
+    column_end = (column % group) // patches
+
+    def one_chunk(index, carry):
+        first = pl.multiple_of(index * chunk, chunk)
+        partner = partner_rows[pl.ds(first, chunk), :].astype(jnp.bfloat16)
+        keys = jnp.dot(partner, key_ref[...], preferred_element_type=jnp.float32)
+        keys = keys.astype(jnp.bfloat16)
+        values = lax.dot_general(
+            value_ref[...], partner, NT, preferred_element_type=jnp.float32
+        ).astype(jnp.bfloat16)
+        for part in range(chunk // group):
+            begin = part * group
+            all_weights = []
+            all_values = []
+            for block in range(width // LANES):
+                cols = slice(block * LANES, (block + 1) * LANES)
+                asked = query_rows[pl.ds(first + begin, group), cols]
+                stacked = jnp.concatenate(
+                    [jnp.where(lane // head_size == s, asked, 0.0) for s in range(side)], axis=0
+                ).astype(jnp.bfloat16)
+                scores = lax.dot_general(
+                    keys[begin : begin + group, cols], stacked, NT,
+                    preferred_element_type=jnp.float32,
+                )
+                packed = jnp.zeros((patches, side * group), jnp.float32)
+                for end in range(group // patches):
+                    packed = jnp.where(
+                        column_end == end, scores[end * patches : (end + 1) * patches], packed
+                    )
+                grown = jnp.exp(packed - jnp.max(packed, axis=0, keepdims=True))
+                weights = grown / jnp.sum(grown, axis=0, keepdims=True)
+                spread = jnp.concatenate(
+                    [jnp.where(column_end == end, weights, 0.0) for end in range(group // patches)],
+                    axis=0,
+                ).astype(jnp.bfloat16)
+                for s in range(side):
+                    head = block * side + s
+                    all_weights.append(spread[:, s * group : (s + 1) * group])
+                    all_values.append(
+                        values[head * channels : (head + 1) * channels, begin : begin + group]
+                    )
+            attended[:, pl.ds(pl.multiple_of(first + begin, group), group)] = jnp.dot(
+                jnp.concatenate(all_values, axis=1),
+                jnp.concatenate(all_weights, axis=0),
+                preferred_element_type=jnp.float32,
+            )
+        return carry
+
+    lax.fori_loop(0, rows // chunk, one_chunk, 0)
+
+    own_rows = base_ref.shape[1]
+    target = lax.broadcasted_iota(jnp.int32, (own_rows, rows), 0)
+    owner_map = jnp.where(target == place_ref[...], 1.0, 0.0).astype(jnp.bfloat16)
+    base = sum3(jnp.dot(split3(base_ref[...]), owner_map, preferred_element_type=jnp.float32))
+    head_out = base + attended[...]
+    confidence = 1.0 + jnp.exp(head_out[3:4, :])
+    channel = lax.broadcasted_iota(jnp.int32, head_out.shape, 0)
+    result = jnp.where(channel == 3, confidence, confidence * head_out)
+    result = jnp.where(live_ref[...] > 0, result, 0.0)
+    out_ref[...] = sum3(
+        lax.dot_general(split3(result), owner_map, NT, preferred_element_type=jnp.float32)
+    )
+
+
+def look_up(owner_row, ids, img_dev):
+    span = min(TABLE, owner_row.shape[0])
+    table = owner_row.reshape(-1, span)
+    parts = jnp.concatenate([table // img_dev, table % img_dev], axis=0).astype(jnp.bfloat16)
+    hot = ids[None, :] % span == jnp.arange(span, dtype=jnp.int32)[:, None]
+    found = jnp.dot(parts, hot.astype(jnp.bfloat16), preferred_element_type=jnp.float32)
+    found = found.reshape(2, -1, ids.shape[0])
+    pick = jnp.arange(found.shape[1], dtype=jnp.int32)[:, None] == ids[None, :] // span
+    found = jnp.sum(jnp.where(pick[None], found, 0.0), axis=1).astype(jnp.int32)
+    return found[0], found[1]
+
+
+def by_owner(
+    tokens, w_embed, w_query, w_key, w_value, w_out, w_head, pair_images, pair_counts, owner_row
+):
+    img_dev, patches, enc_width = tokens.shape
+    dec_width, channels = w_head.shape
+    owners = lax.axis_size("img")
+    groups = lax.axis_size("grp")
+    pair_cap = pair_images.shape[2]
+    my_chip = lax.axis_index("img")
+    my_group = lax.axis_index("grp")
+    head_size = dec_width // HEADS
+    own_rows = img_dev * patches
+    share = img_dev // groups
+    embedded = jnp.dot(
+        tokens.reshape(own_rows, enc_width), w_embed, preferred_element_type=jnp.float32
+    ).astype(jnp.bfloat16)
+    normed = layer_norm(embedded.astype(jnp.float32)).astype(jnp.bfloat16)
+    outgoing = lax.dynamic_slice_in_dim(
+        normed.reshape(img_dev, patches, dec_width), my_group * share, share, 0
+    )
+    everyone = lax.all_gather(outgoing, ("img", "grp"), axis=0, tiled=True)
+
+    queries = jnp.dot(normed, w_query, preferred_element_type=jnp.float32)
+    queries = queries.astype(jnp.bfloat16).astype(jnp.float32) / math.sqrt(head_size)
+    wide = -(-channels // 8) * 8
+    head_weight = jnp.pad(w_head, ((0, 0), (0, wide - channels)))
+    base = lax.dot_general(
+        head_weight, embedded, (((0,), (1,)), ((), ())), preferred_element_type=jnp.float32
+    )
+    out_head = jnp.dot(w_out, head_weight, preferred_element_type=jnp.float32)
+    value_head = jnp.einsum(
+        "hdc,ihd->hci",
+        out_head.reshape(HEADS, head_size, wide),
+        w_value.astype(jnp.float32).reshape(dec_width, HEADS, head_size),
+        precision=lax.Precision.HIGHEST,
+        preferred_element_type=jnp.float32,
+    )
+    value_head = value_head.reshape(HEADS * wide, dec_width).astype(jnp.bfloat16)
+
+    end_count = groups * pair_cap * 2
+    sides = [pair_images[..., s].reshape(owners, groups * pair_cap) for s in range(2)]
+    ids = jnp.concatenate(sides, axis=1)
+    owner, local = look_up(owner_row, ids.reshape(-1), img_dev)
+    owner = owner.reshape(owners, end_count)
+    local = local.reshape(owners, end_count)
+    image_row = owner * img_dev + local
+    half = end_count // 2
+    partner = jnp.concatenate([image_row[:, half:], image_row[:, :half]], axis=1)
+    live = jnp.arange(pair_cap, dtype=jnp.int32)[None, None, :] < pair_counts[:, :, None]
+    live = live.reshape(owners, half).astype(jnp.int32)
+    live = jnp.concatenate([live, live], axis=1)
+    packed = (partner * img_dev + local) * 2 + live
+    mine = owner == my_chip
+    end_index = jnp.arange(end_count, dtype=jnp.int32)
+    earlier = (end_index[:, None] < end_index[None, :]).astype(jnp.bfloat16)
+    ranked = jnp.dot(mine.astype(jnp.bfloat16), earlier, preferred_element_type=jnp.float32)
+    slot_cap = end_count // owners // groups
+    slot = my_group * slot_cap + jnp.arange(slot_cap, dtype=jnp.int32)
+    matched = mine[:, None, :] & (ranked.astype(jnp.int32)[:, None, :] == slot[None, :, None])
+    chosen = jnp.sum(jnp.where(matched, packed[:, None, :], 0), axis=2).reshape(-1)
+    ends = chosen.shape[0]
+    chosen_live = chosen % 2
+    chosen_local = (chosen // 2) % img_dev
+    chosen_partner = chosen // (2 * img_dev)
+    place = chosen_local[:, None] * patches + jnp.arange(patches, dtype=jnp.int32)[None, :]
+    live_rows = jnp.broadcast_to(chosen_live[:, None], (ends, patches)).reshape(1, -1)
+
+    smem = pl.BlockSpec(memory_space=pltpu.SMEM)
+    vmem = pl.BlockSpec(memory_space=pltpu.VMEM)
+    rows = ends * patches
+    totals = pl.pallas_call(
+        functools.partial(decode_kernel, HEADS),
+        out_shape=jax.ShapeDtypeStruct((wide, own_rows), jnp.float32),
+        in_specs=[smem, smem] + [vmem] * 7,
+        out_specs=vmem,
+        scratch_shapes=[
+            pltpu.VMEM((rows, dec_width), jnp.float32),
+            pltpu.VMEM((rows, dec_width), jnp.float32),
+            pltpu.VMEM((wide, rows), jnp.float32),
+        ],
+        compiler_params=pltpu.CompilerParams(vmem_limit_bytes=40 * 2**20),
+    )(
+        chosen_partner, chosen_local, everyone, queries, w_key, value_head, base,
+        place.reshape(1, -1), live_rows,
+    )
+    totals = lax.psum(totals, "grp")
+    totals = totals[:channels].reshape(channels, img_dev, patches).transpose(1, 0, 2)
+    return join(totals, patches, channels)
+
+
+def per_device(tokens, w_embed, w_query, *others):
+    images = tokens.shape[0] * lax.axis_size("img")
+    gathered = images * tokens.shape[1] * w_query.shape[0] * 2
+    run = by_owner if gathered <= GATHER_LIMIT else by_executor
+    return run(tokens, w_embed, w_query, *others)
+
+
 def solution(mesh):
     in_specs = (P("img", None, None), P(), P(), P(), P(), P(), P(), P(), P(), P())
     out_specs = (P("img", None), P("img", None))

time: 280 us -> 107 us (0.38)
  matrix products: 86.3 us -> 6.81 us
  local copies, waits for them, and re-layouts: 67.2 us -> 10.4 us
  other arithmetic: 27.4 us -> 1.35 us
  starting transfers between devices: 23.5 us -> 0.04 us
  between operations: 1.71 us -> 14.3 us
  Pallas kernels: 0 us -> 6.78 us
  waiting for transfers between devices: 66.5 us -> 63.5 us
    dot_general x51 -> x7, matrix products: 75.6 us -> 6.81 us  [the longest x1 2.01 us: by_owner(): jnp.einsum('hdc,ihd->hci', out_head.reshape(HEADS, head_size, wide), w_va...]
    all_to_all x2 -> x0, waiting for transfers between devices: 66.5 us -> none  [the longest x1 58.2 us: per_device(): lax.all_to_all(outgoing, 'img', split_axis=0, concat_axis=0, tiled=True)]
    all_gather x0 -> x1, waiting for transfers between devices: none -> 63.5 us  [by_owner(): everyone = lax.all_gather(outgoing, ('img', 'grp'), axis=0, tiled=True)]
    gather x3 -> x0, local copies, waits for them, and re-layouts: 32 us -> none  [the longest x1 25.9 us: per_device(): token_rows = owner_row[pair_images].reshape(owners, end_count)]
    all_to_all x2 -> x0, starting transfers between devices: 23.5 us -> none  [the longest x1 15 us: per_device(): lax.all_to_all(outgoing_back.reshape(owners, slot_cap, -1), 'img', split_...]
    reshape x44 -> x5, local copies, waits for them, and re-layouts: 12.2 us -> 0.49 us  [the longest x1 0.14 us: by_owner(): totals[:channels].reshape(channels, img_dev, patches).transpose(1, 0, 2)]
    sub x8 -> x0, matrix products: 10.6 us -> none  [decode_block(): weights = jax.nn.softmax(scores, axis=-1).astype(jnp.bfloat16)]
    convert_element_type x8 -> x0, local copies, waits for them, and re-layouts: 9.6 us -> none  [decode_block(): attended.astype(jnp.bfloat16)]
  transfers between devices with their start and end apart: 2 -> 1, of which waited for: 2 -> 1; matrix products, arithmetic and copies ran while one was open for 1% -> 8% of each run, Pallas kernels for 0% -> 0%
where the time goes in v1:
time: 107 us
  waiting for transfers between devices  63.5 us (59%)
  between operations  14.3 us (13%)
  local copies, waits for them, and re-layouts  10.4 us (10%)
  matrix products  6.81 us (6%)
  Pallas kernels  6.78 us (6%)
  blocking collectives  3.52 us (3%)
  other arithmetic  1.35 us (1%)
    all_gather x1, waiting for transfers between devices, by_owner(): everyone = lax.all_gather(outgoing, ('img', 'grp'), axis=0, tiled=True)  63.5 us
    unnamed x25, local copies, waits for them, and re-layouts  8.37 us
    pallas_call x1, Pallas kernels, by_owner(): pl.pallas_call(functools.partial(decode_kernel, HEADS), out_shape=jax.Sha...  6.78 us
    psum x1, blocking collectives, by_owner(): totals = lax.psum(totals, 'grp')  3.52 us
  transfers between devices with their start and end apart: 1, of which 1 were waited for; matrix products, arithmetic and copies ran while one was open for 8% of the time, Pallas kernels for 0%

profile of v1, /device:TPU:0, one launch (start us, length us, event | category | flops | bytes accessed | tf_op | source)
XLA Modules:
  0.0 106.8 jit_solution(5568630271981693948)
XLA Ops:
  7.2 0.0 copy-start
  7.2 0.0 all-gather.2.cloned.1.call-start
  7.2 1.3 %copy-done = bf16[1024,768]{1,0:T(8,128)(2,1)S(1)} copy-done((bf16[1024,768]{1,0:T(8,128)(2,1)S(1)}, bf16[1024,768]{1,0:T(8,128)(2,1)}, u32[]{:S(2)}) %copy-start) | copy-done | bytes 1572888
  8.6 1.7 %convert_reduce_fusion = (f32[256]{0:T(256)S(1)}, bf16[256,768]{1,0:T(8,128)(2,1)S(1)}) fusion(bf16[1024,768]{1,0:T(8,128)(2,1)S(1)} %copy-done, bf16[32,8,1024]{2,1,0:T(8,128)(2,1)} %param.10), kind=kOutput, calls=%fused_computation.11 | convolution fusion | flops 403242752 | bytes 2491392 | tf_op jit(solution)/shard_map/dot_general | solution.py:291
  10.3 0.0 copy-start.7
  10.3 0.0 copy-start.8
  10.3 0.2 fusion.6
  10.6 0.2 fusion.31
  10.8 0.7 constant_dynamic-slice_fusion
  11.5 0.0 all-gather.2.cloned.1.call-update
  11.5 0.1 lt.67
  11.6 0.0 copy-done.9
  11.6 0.1 copy.62
  11.7 0.1 lt.69
  11.8 0.1 lt.70
  11.8 0.0 copy-done.7
  11.8 0.1 slice_reduce_fusion.2
  12.0 0.1 reshape_squeeze.10
  12.0 0.1 reshape_squeeze.11
  12.1 0.0 copy-done.8
  12.2 0.4 fusion
  12.7 0.1 select_reduce_fusion.1
  12.8 0.1 compare_reduce_fusion
  12.9 0.0 copy-start.3
  12.9 0.1 multiply_reduce_fusion
  13.1 0.2 convolution_convert_fusion.3
  13.3 0.4 select_reduce_fusion
  13.7 0.1 reshape.307
  13.8 0.1 iota_add_fusion
  13.9 0.1 add.134.place_ref
  14.0 0.1 broadcast_in_dim.30
  14.1 0.1 reshape.312.live_ref
  14.2 1.7 %convolution_bitcast_fusion = f32[768,32]{0,1:T(8,128)S(1)} fusion(bf16[768,768]{1,0:T(8,128)(2,1)} %param.15, bf16[768,28]{0,1:T(8,128)(2,1)S(1)} %copy-done.5), kind=kOutput, calls=%fused_computation.7 | convolution fusion | flops 37748736 | bytes 1320960 | tf_op jit(solution)/shard_map/dot_general | solution.py:307
  15.9 0.1 reshape.310
  16.1 0.0 copy-start.6
  16.1 1.5 %copy.63 = bf16[768,768]{0,1:T(8,128)(2,1)} copy(bf16[768,768]{1,0:T(8,128)(2,1)S(1)} %copy-done.3) | data formatting | bytes 2359296 | tf_op args[4]
  17.5 0.3 fusion.11.base_ref
  17.8 2.0 %convolution_convert_fusion = bf16[12,32,768]{2,1,0:T(8,128)(2,1)S(1)} fusion(bf16[768,12,64]{0,2,1:T(8,128)(2,1)} %bitcast.54, f32[12,64,32]{1,0,2:T(8,128)S(1)} %reshape.310), kind=kOutput, calls=%fused_computation.2 | convolution fusion | flops 226787328 | bytes 1867776 | tf_op jit(solution)/shard_map/hdc,ihd->hci/dot_general | solution.py:308
  19.8 0.5 fusion.2.query_ref
  20.3 63.5 %all-gather.2.cloned.1.call-done.normed_ref = bf16[512,8,768]{2,1,0:T(8,128)(2,1)} async-done(((bf16[16,8,768]{2,1,0:T(8,128)(2,1)}), bf16[512,8,768]{2,1,0:T(8,128)(2,1)}) %all-gather.2.cloned.1.call-update) | async-done | bytes 6291472 | tf_op jit(solution)/shard_map/all_gather | solution.py:298
  83.9 2.8 %copy-done.1 = bf16[512,8,768]{2,1,0:T(8,128)(2,1)S(1)} copy-done((bf16[512,8,768]{2,1,0:T(8,128)(2,1)S(1)}, bf16[512,8,768]{2,1,0:T(8,128)(2,1)}, u32[]{:S(2)}) %copy-start.1) | copy-done | bytes 6291480
  86.7 1.3 %copy-done.2 = bf16[768,768]{1,0:T(8,128)(2,1)S(1)} copy-done((bf16[768,768]{1,0:T(8,128)(2,1)S(1)}, bf16[768,768]{1,0:T(8,128)(2,1)}, u32[]{:S(2)}) %copy-start.2) | copy-done | bytes 1179672
  87.9 6.8 %shard_map.113 = f32[32,256]{1,0:T(8,128)S(1)} custom-call(s32[128]{0:T(128)S(1)} %get-tuple-element.27.source_ref, s32[128]{0:T(128)S(1)} %get-tuple-element.17.local_ref, bf16[512,8,768]{2,1,0:T(8,128)(2,1)S(1)} %copy-done.1, f32[256,768]{1,0:T(8,128)S(1)} %fusion.2.query_ref, bf16[768,768]{1,0:T(8,128)(2,1)S(1)} %copy-done.2, ...), custom_call_target="tpu_custom_call" | custom-call | tf_op jit(solution)/shard_map/pallas_call | solution.py:348
  94.7 3.5 %psum.7 = f32[32,256]{1,0:T(8,128)S(1)} all-reduce(f32[32,256]{1,0:T(8,128)S(1)} %shard_map.113), channel_id=1, replica_groups=mesh['img'=16,'grp'=2] {'grp'}, use_global_device_ids=true, to_apply=%region_4.5 | all-reduce | flops 8192 | bytes 65536 | tf_op jit(solution)/shard_map/psum | solution.py:363
  98.2 0.1 copy.65
  98.4 0.1 copy.66
  98.5 0.7 copy.68
  99.2 0.7 copy.67
  (32 shorter events, 0.3 us)
Async XLA Ops:
  7.2 1.4 %copy-start = (bf16[1024,768]{1,0:T(8,128)(2,1)S(1)}, bf16[1024,768]{1,0:T(8,128)(2,1)}, u32[]{:S(2)}) copy-start(bf16[1024,768]{1,0:T(8,128)(2,1)} %param.11) | copy-start | bytes 4718596
  7.2 76.7 %all-gather.2.cloned.1.call-start = ((), (), s32[]{:S(2)}) async-start(), calls=%async_computation | async-start | bytes 6488064 | tf_op jit(solution)/shard_map/all_gather | solution.py:298
  10.3 1.3 %copy-start.9 = (s32[16,2]{0,1:T(2,128)S(1)}, s32[16,2]{0,1:T(2,128)}, u32[]{:S(2)}) copy-start(s32[16,2]{0,1:T(2,128)} %param.18) | copy-start | bytes 388
  10.3 1.6 %copy-start.7 = (s32[16,2,64,2]{2,3,1,0:T(2,128)S(1)}, s32[16,2,64,2]{2,3,1,0:T(2,128)}, u32[]{:S(2)}) copy-start(s32[16,2,64,2]{2,3,1,0:T(2,128)} %param.17) | copy-start | bytes 49156
  10.3 1.9 %copy-start.8 = (s32[512]{0:T(512)S(1)}, s32[512]{0:T(512)}, u32[]{:S(2)}) copy-start(s32[512]{0:T(512)} %param.19) | copy-start | bytes 6148
  11.5 2.7 %copy-start.5 = (bf16[768,28]{0,1:T(8,128)(2,1)S(1)}, bf16[768,28]{0,1:T(8,128)(2,1)}, u32[]{:S(2)}) copy-start(bf16[768,28]{0,1:T(8,128)(2,1)} %param.16) | copy-start | bytes 129028
  12.9 3.1 %copy-start.3 = (bf16[768,768]{1,0:T(8,128)(2,1)S(1)}, bf16[768,768]{1,0:T(8,128)(2,1)}, u32[]{:S(2)}) copy-start(bf16[768,768]{1,0:T(8,128)(2,1)} %param.14) | copy-start | bytes 3538948
  16.1 1.5 %copy-start.6 = (bf16[768,28]{0,1:T(8,128)(2,1)S(1)}, bf16[768,28]{0,1:T(8,128)(2,1)}, u32[]{:S(2)}) copy-start(bf16[768,28]{0,1:T(8,128)(2,1)} %param.16) | copy-start | bytes 129028
  17.5 2.3 %copy-start.4 = (bf16[768,768]{1,0:T(8,128)(2,1)S(1)}, bf16[768,768]{1,0:T(8,128)(2,1)}, u32[]{:S(2)}) copy-start(bf16[768,768]{1,0:T(8,128)(2,1)} %param.12) | copy-start | bytes 3538948
  83.9 2.8 %copy-start.1 = (bf16[512,8,768]{2,1,0:T(8,128)(2,1)S(1)}, bf16[512,8,768]{2,1,0:T(8,128)(2,1)}, u32[]{:S(2)}) copy-start(bf16[512,8,768]{2,1,0:T(8,128)(2,1)} %all-gather.2.cloned.1.call-done.normed_ref) | copy-start | bytes 18874372
  86.7 1.3 %copy-start.2 = (bf16[768,768]{1,0:T(8,128)(2,1)S(1)}, bf16[768,768]{1,0:T(8,128)(2,1)}, u32[]{:S(2)}) copy-start(bf16[768,768]{1,0:T(8,128)(2,1)} %key_ref.1) | copy-start | bytes 3538948
Sparse Core Ops, SparseCore 0:
  11.6 72.2 all-gather.1

commit v2 on v1

--- a/solution.py
+++ b/solution.py
@@ -263,6 +263,175 @@
     )
 
 
+def gather_kernel(
+    depth, own_ref, all_ref, place_sem, send_sem, recv_sem, mate_send_sem, mate_recv_sem
+):
+    share = own_ref.shape[0]
+    me = lax.axis_index("img")
+    core = lax.axis_index("grp")
+    layer = me // 4
+    tall = me // 2 % 2
+    wide = me % 2
+    mesh_ids = pl.DeviceIdType.MESH
+
+    def chip(z, y, x):
+        return z * 4 + y * 2 + x
+
+    def slot(unit):
+        return all_ref.at[pl.ds((unit * 2 + core) * share, share)]
+
+    def copy(unit, way, target, source=None):
+        return pltpu.make_async_remote_copy(
+            src_ref=slot(unit) if source is None else source,
+            dst_ref=slot(unit),
+            send_sem=send_sem.at[way, unit],
+            recv_sem=recv_sem.at[unit],
+            device_id={"img": target, "grp": core},
+            device_id_type=mesh_ids,
+        )
+
+    def mate_copy(unit, source=None):
+        return pltpu.make_async_remote_copy(
+            src_ref=slot(unit) if source is None else source,
+            dst_ref=slot(unit),
+            send_sem=mate_send_sem.at[unit],
+            recv_sem=mate_recv_sem.at[unit],
+            device_id={"img": me, "grp": 1 - core},
+            device_id_type=mesh_ids,
+        )
+
+    across = chip(layer, tall, 1 - wide)
+    along = chip(layer, 1 - tall, wide)
+    has = {1: layer < depth - 1, -1: layer > 0}
+
+    barrier = pltpu.get_barrier_semaphore()
+    for target in (across, along):
+        pl.semaphore_signal(
+            barrier, inc=1, device_id={"img": target, "grp": core}, device_id_type=mesh_ids
+        )
+    pl.semaphore_signal(
+        barrier, inc=1, device_id={"img": me, "grp": 1 - core}, device_id_type=mesh_ids
+    )
+    for sign in (1, -1):
+        @pl.when(has[sign])
+        def _():
+            pl.semaphore_signal(
+                barrier,
+                inc=1,
+                device_id={"img": me + 4 * sign, "grp": core},
+                device_id_type=mesh_ids,
+            )
+    pl.semaphore_wait(
+        barrier, 3 + has[1].astype(jnp.int32) + has[-1].astype(jnp.int32)
+    )
+
+    def run(action):
+        def at(distance, sign, body):
+            z = layer + sign * distance
+            if distance == 0:
+                body(z)
+            else:
+                pl.when((z >= 0) & (z < depth))(lambda: body(z))
+
+        for step in range(depth + 2):
+            for sign in (1, -1):
+                if step < depth and (step > 0 or sign == 1):
+                    def column(z):
+                        unit = chip(z, tall, wide)
+                        own = own_ref if step == 0 else None
+                        if step > 0:
+                            action("arrive", lambda: copy(unit, 0, across))
+                        for onward in (1, -1):
+                            if step == 0 or onward == -sign:
+                                @pl.when(has[onward])
+                                def _():
+                                    action(
+                                        "send",
+                                        lambda: copy(unit, 0 if onward == 1 else 1, me + 4 * onward, own),
+                                    )
+                        action("send", lambda: copy(unit, 2, across, own))
+                        action("send", lambda: copy(unit, 3, along, own))
+                        action("send", lambda: mate_copy(unit, own))
+
+                    at(step, sign, column)
+                back = step - 1
+                if 0 <= back < depth and (back > 0 or sign == 1):
+                    def beside(z):
+                        unit = chip(z, tall, 1 - wide)
+                        action("arrive", lambda: copy(unit, 0, across))
+                        @pl.when(z % 2 == 1)
+                        def _():
+                            action("send", lambda: copy(unit, 3, along))
+                        action("send", lambda: mate_copy(unit))
+                        unit_up = chip(z, 1 - tall, wide)
+                        action("arrive", lambda: copy(unit_up, 0, across))
+                        @pl.when(z % 2 == 0)
+                        def _():
+                            action("send", lambda: copy(unit_up, 2, across))
+                        action("send", lambda: mate_copy(unit_up))
+
+                    at(back, sign, beside)
+                back2 = step - 2
+                if 0 <= back2 < depth and (back2 > 0 or sign == 1):
+                    def opposite(z):
+                        unit = chip(z, 1 - tall, 1 - wide)
+                        action("arrive", lambda: copy(unit, 0, across))
+                        action("send", lambda: mate_copy(unit))
+
+                    at(back2, sign, opposite)
+
+    def begin(kind, descriptor):
+        if kind == "send":
+            descriptor().start()
+        else:
+            descriptor().wait_recv()
+
+    def finish(kind, descriptor):
+        if kind == "send":
+            descriptor().wait_send()
+
+    place = pltpu.make_async_copy(own_ref, slot(me), place_sem)
+    place.start()
+    run(begin)
+    run(finish)
+    place.wait()
+
+    def from_mate(unit, carry):
+        theirs = all_ref.at[pl.ds((unit * 2 + 1 - core) * share, share)]
+        pltpu.make_async_remote_copy(
+            src_ref=theirs,
+            dst_ref=theirs,
+            send_sem=mate_send_sem.at[unit],
+            recv_sem=mate_recv_sem.at[unit],
+            device_id={"img": me, "grp": 1 - core},
+            device_id_type=mesh_ids,
+        ).wait_recv()
+        return carry
+
+    lax.fori_loop(0, 4 * depth, from_mate, 0)
+
+
+def gather_rows(outgoing, owners):
+    share, patches, width = outgoing.shape
+    vmem = pl.BlockSpec(memory_space=pltpu.VMEM)
+    return pl.pallas_call(
+        functools.partial(gather_kernel, owners // 4),
+        out_shape=jax.ShapeDtypeStruct((owners * 2 * share, patches, width), outgoing.dtype),
+        in_specs=[vmem],
+        out_specs=vmem,
+        scratch_shapes=[
+            pltpu.SemaphoreType.DMA,
+            pltpu.SemaphoreType.DMA((4, owners)),
+            pltpu.SemaphoreType.DMA((owners,)),
+            pltpu.SemaphoreType.DMA((owners,)),
+            pltpu.SemaphoreType.DMA((owners,)),
+        ],
+        compiler_params=pltpu.CompilerParams(
+            collective_id=0, has_side_effects=True, vmem_limit_bytes=24 * 2**20
+        ),
+    )(outgoing)
+
+
 def look_up(owner_row, ids, img_dev):
     span = min(TABLE, owner_row.shape[0])
     table = owner_row.reshape(-1, span)
@@ -295,7 +464,7 @@
     outgoing = lax.dynamic_slice_in_dim(
         normed.reshape(img_dev, patches, dec_width), my_group * share, share, 0
     )
-    everyone = lax.all_gather(outgoing, ("img", "grp"), axis=0, tiled=True)
+    everyone = gather_rows(outgoing, owners)
 
     queries = jnp.dot(normed, w_query, preferred_element_type=jnp.float32)
     queries = queries.astype(jnp.bfloat16).astype(jnp.float32) / math.sqrt(head_size)

time: 107 us -> 63.4 us (0.59)
  waiting for transfers between devices: 63.5 us -> 0 us
  Pallas kernels: 6.78 us -> 43.5 us
  between operations: 14.3 us -> 0.93 us
  local copies, waits for them, and re-layouts: 10.4 us -> 7.21 us
  matrix products: 6.81 us -> 5.69 us
    all_gather x1 -> x0, waiting for transfers between devices: 63.5 us -> none  [by_owner(): everyone = lax.all_gather(outgoing, ('img', 'grp'), axis=0, tiled=True)]
    pallas_call x0 -> x1, Pallas kernels: none -> 36.7 us  [gather_rows(): pl.pallas_call(functools.partial(gather_kernel, owners // 4), out_shape=j...]
    unnamed x25 -> x15, local copies, waits for them, and re-layouts: 8.37 us -> 5.05 us
  transfers between devices with their start and end apart: 1 -> 0, of which waited for: 1 -> 0; matrix products, arithmetic and copies ran while one was open for 8% -> 0% of each run, Pallas kernels for 0% -> 0%
where the time goes in v2:
time: 63.4 us; the launch traced here: 63.1 us
  Pallas kernels  43.5 us (69%)
  local copies, waits for them, and re-layouts  7.21 us (11%)
  matrix products  5.69 us (9%)
  blocking collectives  3.57 us (6%)
  other arithmetic  2.18 us (3%)
  between operations  0.93 us (1%)
    pallas_call x1, Pallas kernels, gather_rows(): pl.pallas_call(functools.partial(gather_kernel, owners // 4), out_shape=j...  36.7 us
    pallas_call x1, Pallas kernels, by_owner(): pl.pallas_call(functools.partial(decode_kernel, HEADS), out_shape=jax.Sha...  6.78 us
    unnamed x15, local copies, waits for them, and re-layouts  5.05 us
    psum x1, blocking collectives, by_owner(): totals = lax.psum(totals, 'grp')  3.57 us
    dot_general x1, matrix products, by_owner(): jnp.einsum('hdc,ihd->hci', out_head.reshape(HEADS, head_size, wide), w_va...  1.91 us
    dot_general x1, matrix products, by_owner(): out_head = jnp.dot(w_out, head_weight, preferred_element_type=jnp.float32)  1.77 us

profile of v2, /device:TPU:0, one launch (start us, length us, event | category | flops | bytes accessed | tf_op | source)
XLA Modules:
  0.0 63.1 jit_solution(3038042709059815927)
XLA Ops:
  0.6 0.0 copy-start
  0.7 0.1 lt.67
  0.8 0.8 %fusion.19 = (bf16[4,128]{1,0:T(4,128)(2,1)S(1)}, bf16[4,128]{1,0:T(4,128)(2,1)S(1)}) fusion(s32[512]{0:T(512)} %param.19), kind=kLoop, calls=%fused_computation.58 | loop fusion | flops 10752 | bytes 4096 | tf_op jit(solution)/shard_map/convert.1
  1.5 0.8 %copy.62 = s32[16,2]{1,0:T(8,128)S(1)} copy(s32[16,2]{0,1:T(2,128)} %param.18) | data formatting | bytes 256 | tf_op args[8]
  2.3 0.1 lt.69
  2.4 0.1 lt.70
  2.5 0.9 %slice_reduce_fusion.2 = (s32[16,2,64]{2,1,0:T(2,128)S(1)}, s32[16,2,64]{2,1,0:T(2,128)S(1)}) fusion(s32[16,2,64,2]{2,3,1,0:T(2,128)} %param.17), kind=kLoop, calls=%fused_computation.44 | loop fusion | bytes 32768 | tf_op jit(solution)/shard_map/slice | solution.py:487
  3.4 0.1 reshape_squeeze.10
  3.5 0.1 reshape_squeeze.11
  3.7 1.8 %convolution_bitcast_fusion = f32[768,32]{0,1:T(8,128)S(1)} fusion(bf16[768,768]{1,0:T(8,128)(2,1)} %param.15, bf16[768,28]{0,1:T(8,128)(2,1)} %param.16), kind=kOutput, calls=%fused_computation.7 | convolution fusion | flops 37748736 | bytes 1320960 | tf_op jit(solution)/shard_map/dot_general | solution.py:476
  5.4 0.0 copy-start.4
  5.4 0.4 fusion
  5.9 0.1 select_reduce_fusion.1
  6.1 0.1 compare_reduce_fusion
  6.1 0.1 multiply_reduce_fusion
  6.3 0.2 convolution_convert_fusion.3
  6.5 0.4 select_reduce_fusion
  6.9 0.1 reshape.307
  7.0 0.1 iota_add_fusion
  7.1 0.1 add.134.place_ref
  7.2 0.1 broadcast_in_dim.30
  7.3 0.1 reshape.312.live_ref
  7.4 0.1 reshape.310
  7.5 0.0 copy-done
  7.5 0.0 copy-done.4
  7.5 0.0 copy-start.3
  7.5 0.7 %convert_reduce_fusion = (f32[256]{0:T(256)S(1)}, bf16[256,768]{1,0:T(8,128)(2,1)S(1)}) fusion(bf16[1024,768]{1,0:T(8,128)(2,1)S(1)} %copy-done, bf16[32,8,1024]{2,1,0:T(8,128)(2,1)S(1)} %copy-done.4), kind=kOutput, calls=%fused_computation.11 | convolution fusion | flops 403242752 | bytes 2491392 | tf_op jit(solution)/shard_map/dot_general | solution.py:460
  8.2 0.0 copy-start.2
  8.2 0.2 fusion.6
  8.5 0.0 copy-done.3
  8.5 0.2 fusion.11.base_ref
  8.7 0.2 fusion.31
  9.0 0.5 copy-done.2
  9.5 0.5 fusion.2.query_ref
  10.0 2.4 %copy.63 = bf16[768,768]{0,1:T(8,128)(2,1)} copy(bf16[768,768]{1,0:T(8,128)(2,1)} %param.14) | data formatting | bytes 2359296 | tf_op args[4]
  12.4 1.9 %convolution_convert_fusion = bf16[12,32,768]{2,1,0:T(8,128)(2,1)S(1)} fusion(bf16[768,12,64]{0,2,1:T(8,128)(2,1)} %bitcast.54, f32[12,64,32]{1,0,2:T(8,128)S(1)} %reshape.310), kind=kOutput, calls=%fused_computation.2 | convolution fusion | flops 226787328 | bytes 1867776 | tf_op jit(solution)/shard_map/hdc,ihd->hci/dot_general | solution.py:477
  14.3 0.0 copy-start.1
  14.3 36.7 %shard_map.113.normed_ref = bf16[512,8,768]{2,1,0:T(8,128)(2,1)S(1)} custom-call(bf16[16,8,768]{2,1,0:T(8,128)(2,1)S(1)} %constant_dynamic-slice_fusion.own_ref), custom_call_target="tpu_custom_call" | custom-call | tf_op jit(solution)/shard_map/pallas_call | solution.py:417
  51.0 0.0 copy-done.1
  51.0 6.8 %shard_map.114 = f32[32,256]{1,0:T(8,128)S(1)} custom-call(s32[128]{0:T(128)S(1)} %get-tuple-element.27.source_ref, s32[128]{0:T(128)S(1)} %get-tuple-element.17.local_ref, bf16[512,8,768]{2,1,0:T(8,128)(2,1)S(1)} %shard_map.113.normed_ref, f32[256,768]{1,0:T(8,128)S(1)} %fusion.2.query_ref, bf16[768,768]{1,0:T(8,128)(2,1)S(1)} %copy-done.1, ...), custom_call_target="tpu_custom_call" | custom-call | tf_op jit(solution)/shard_map/pallas_call | solution.py:517
  57.8 3.6 %psum.7 = f32[32,256]{1,0:T(8,128)S(1)} all-reduce(f32[32,256]{1,0:T(8,128)S(1)} %shard_map.114), channel_id=1, replica_groups=mesh['img'=16,'grp'=2] {'grp'}, use_global_device_ids=true, to_apply=%region_4.5 | all-reduce | flops 8192 | bytes 65536 | tf_op jit(solution)/shard_map/psum | solution.py:532
  61.4 0.1 copy.65
  61.5 0.1 copy.66
  61.7 0.7 %copy.68 = f32[32,192]{1,0:T(8,128)} copy(f32[32,192]{0,1:T(8,128)S(1)} %fusion.10) | data formatting | bytes 49152
  62.4 0.7 %copy.67 = f32[32,32]{1,0:T(8,128)} copy(f32[32,32]{0,1:T(8,128)S(1)} %maximum_bitcast_fusion) | data formatting | bytes 8192
  (23 shorter events, 0.3 us)
Async XLA Ops:
  0.6 6.8 %copy-start = (bf16[1024,768]{1,0:T(8,128)(2,1)S(1)}, bf16[1024,768]{1,0:T(8,128)(2,1)}, u32[]{:S(2)}) copy-start(bf16[1024,768]{1,0:T(8,128)(2,1)} %param.11) | copy-start | bytes 4718596
  5.4 2.1 %copy-start.4 = (bf16[32,8,1024]{2,1,0:T(8,128)(2,1)S(1)}, bf16[32,8,1024]{2,1,0:T(8,128)(2,1)}, u32[]{:S(2)}) copy-start(bf16[32,8,1024]{2,1,0:T(8,128)(2,1)} %param.10) | copy-start | bytes 1572868
  7.5 1.0 %copy-start.3 = (bf16[768,28]{0,1:T(8,128)(2,1)S(1)}, bf16[768,28]{0,1:T(8,128)(2,1)}, u32[]{:S(2)}) copy-start(bf16[768,28]{0,1:T(8,128)(2,1)} %param.16) | copy-start | bytes 129028
  8.2 1.3 %copy-start.2 = (bf16[768,768]{1,0:T(8,128)(2,1)S(1)}, bf16[768,768]{1,0:T(8,128)(2,1)}, u32[]{:S(2)}) copy-start(bf16[768,768]{1,0:T(8,128)(2,1)} %param.12) | copy-start | bytes 3538948
  14.3 36.7 %copy-start.1 = (bf16[768,768]{1,0:T(8,128)(2,1)S(1)}, bf16[768,768]{1,0:T(8,128)(2,1)}, u32[]{:S(2)}) copy-start(bf16[768,768]{1,0:T(8,128)(2,1)} %key_ref.1) | copy-start | bytes 3538948

commit v3 on v2

--- a/solution.py
+++ b/solution.py
@@ -264,7 +264,9 @@
 
 
 def gather_kernel(
-    depth, own_ref, all_ref, place_sem, send_sem, recv_sem, mate_send_sem, mate_recv_sem
+    depth, heads, own_ref, normed_ref, embedded_ref, head_ref, query_hbm, out_hbm, value_hbm,
+    all_ref, query_ref, value_ref, base_ref, weights, weight_sem, place_sem, send_sem, recv_sem,
+    mate_send_sem, mate_recv_sem
 ):
     share = own_ref.shape[0]
     me = lax.axis_index("img")
@@ -273,6 +275,40 @@
     tall = me // 2 % 2
     wide = me % 2
     mesh_ids = pl.DeviceIdType.MESH
+    loads = [
+        pltpu.make_async_copy(source, weights.at[index], weight_sem.at[index])
+        for index, source in enumerate((query_hbm, out_hbm, value_hbm))
+    ]
+    for load in loads:
+        load.start()
+
+    def own_queries():
+        head_size = normed_ref.shape[1] // heads
+        loads[0].wait()
+        asked = jnp.dot(normed_ref[...], weights[0], preferred_element_type=jnp.float32)
+        query_ref[...] = asked.astype(jnp.bfloat16).astype(jnp.float32) / math.sqrt(head_size)
+        base_ref[...] = lax.dot_general(
+            head_ref[...], embedded_ref[...], NT, preferred_element_type=jnp.float32
+        )
+
+    def value_to_head():
+        head_size = normed_ref.shape[1] // heads
+        channels = head_ref.shape[0]
+        loads[1].wait()
+        out_head = lax.dot_general(
+            head_ref[...], weights[1], NT, preferred_element_type=jnp.float32
+        )
+        tiled = jnp.concatenate([out_head] * heads, axis=0)
+        row = lax.broadcasted_iota(jnp.int32, tiled.shape, 0)
+        column = lax.broadcasted_iota(jnp.int32, tiled.shape, 1)
+        tiled = jnp.where(row // channels == column // head_size, tiled, 0.0)
+        high = tiled.astype(jnp.bfloat16)
+        low = (tiled - high.astype(jnp.float32)).astype(jnp.bfloat16)
+        loads[2].wait()
+        value_ref[...] = (
+            lax.dot_general(high, weights[2], NT, preferred_element_type=jnp.float32)
+            + lax.dot_general(low, weights[2], NT, preferred_element_type=jnp.float32)
+        ).astype(jnp.bfloat16)
 
     def chip(z, y, x):
         return z * 4 + y * 2 + x
@@ -325,7 +361,7 @@
         barrier, 3 + has[1].astype(jnp.int32) + has[-1].astype(jnp.int32)
     )
 
-    def run(action):
+    def run(action, between):
         def at(distance, sign, body):
             z = layer + sign * distance
             if distance == 0:
@@ -379,6 +415,8 @@
                         action("send", lambda: mate_copy(unit))
 
                     at(back2, sign, opposite)
+            if step in between:
+                between[step]()
 
     def begin(kind, descriptor):
         if kind == "send":
@@ -392,8 +430,8 @@
 
     place = pltpu.make_async_copy(own_ref, slot(me), place_sem)
     place.start()
-    run(begin)
-    run(finish)
+    run(begin, {0: own_queries, 1: value_to_head})
+    run(finish, {})
     place.wait()
 
     def from_mate(unit, carry):
@@ -411,15 +449,24 @@
     lax.fori_loop(0, 4 * depth, from_mate, 0)
 
 
-def gather_rows(outgoing, owners):
+def gather_rows(outgoing, owners, normed, embedded, head_weight, w_query, w_out, w_value):
     share, patches, width = outgoing.shape
+    wide = head_weight.shape[0]
     vmem = pl.BlockSpec(memory_space=pltpu.VMEM)
+    away = pl.BlockSpec(memory_space=pl.ANY)
     return pl.pallas_call(
-        functools.partial(gather_kernel, owners // 4),
-        out_shape=jax.ShapeDtypeStruct((owners * 2 * share, patches, width), outgoing.dtype),
-        in_specs=[vmem],
-        out_specs=vmem,
+        functools.partial(gather_kernel, owners // 4, HEADS),
+        out_shape=(
+            jax.ShapeDtypeStruct((owners * 2 * share, patches, width), outgoing.dtype),
+            jax.ShapeDtypeStruct(normed.shape, jnp.float32),
+            jax.ShapeDtypeStruct((HEADS * wide, width), jnp.bfloat16),
+            jax.ShapeDtypeStruct((wide, normed.shape[0]), jnp.float32),
+        ),
+        in_specs=[vmem] * 4 + [away] * 3,
+        out_specs=(vmem,) * 4,
         scratch_shapes=[
+            pltpu.VMEM((3, width, width), jnp.bfloat16),
+            pltpu.SemaphoreType.DMA((3,)),
             pltpu.SemaphoreType.DMA,
             pltpu.SemaphoreType.DMA((4, owners)),
             pltpu.SemaphoreType.DMA((owners,)),
@@ -427,9 +474,9 @@
             pltpu.SemaphoreType.DMA((owners,)),
         ],
         compiler_params=pltpu.CompilerParams(
-            collective_id=0, has_side_effects=True, vmem_limit_bytes=24 * 2**20
+            collective_id=0, has_side_effects=True, vmem_limit_bytes=32 * 2**20
         ),
-    )(outgoing)
+    )(outgoing, normed, embedded, head_weight, w_query, w_out, w_value)
 
 
 def look_up(owner_row, ids, img_dev):
@@ -454,7 +501,6 @@
     pair_cap = pair_images.shape[2]
     my_chip = lax.axis_index("img")
     my_group = lax.axis_index("grp")
-    head_size = dec_width // HEADS
     own_rows = img_dev * patches
     share = img_dev // groups
     embedded = jnp.dot(
@@ -464,24 +510,11 @@
     outgoing = lax.dynamic_slice_in_dim(
         normed.reshape(img_dev, patches, dec_width), my_group * share, share, 0
     )
-    everyone = gather_rows(outgoing, owners)
-
-    queries = jnp.dot(normed, w_query, preferred_element_type=jnp.float32)
-    queries = queries.astype(jnp.bfloat16).astype(jnp.float32) / math.sqrt(head_size)
     wide = -(-channels // 8) * 8
-    head_weight = jnp.pad(w_head, ((0, 0), (0, wide - channels)))
-    base = lax.dot_general(
-        head_weight, embedded, (((0,), (1,)), ((), ())), preferred_element_type=jnp.float32
-    )
-    out_head = jnp.dot(w_out, head_weight, preferred_element_type=jnp.float32)
-    value_head = jnp.einsum(
-        "hdc,ihd->hci",
-        out_head.reshape(HEADS, head_size, wide),
-        w_value.astype(jnp.float32).reshape(dec_width, HEADS, head_size),
-        precision=lax.Precision.HIGHEST,
-        preferred_element_type=jnp.float32,
-    )
-    value_head = value_head.reshape(HEADS * wide, dec_width).astype(jnp.bfloat16)
+    head_weight = jnp.pad(w_head.T, ((0, wide - channels), (0, 0)))
+    everyone, queries, value_head, base = gather_rows(
+        outgoing, owners, normed, embedded, head_weight, w_query, w_out, w_value
+    )
 
     end_count = groups * pair_cap * 2
     sides = [pair_images[..., s].reshape(owners, groups * pair_cap) for s in range(2)]

time: 63.4 us -> 70.4 us (1.11)
  local copies, waits for them, and re-layouts: 7.21 us -> 17.3 us
  matrix products: 5.69 us -> 1.26 us
    unnamed x15 -> x32, local copies, waits for them, and re-layouts: 5.05 us -> 14.3 us
    dot_general x4 -> x0, matrix products: 4.42 us -> none  [the longest x1 1.91 us: by_owner(): jnp.einsum('hdc,ihd->hci', out_head.reshape(HEADS, head_size, wide), w_va...]
    pad x0 -> x1, local copies, waits for them, and re-layouts: none -> 0.93 us  [by_owner(): head_weight = jnp.pad(w_head.T, ((0, wide - channels), (0, 0)))]
    pallas_call x1, Pallas kernels: 36.7 us -> 37.4 us  [gather_rows(): pl.pallas_call(functools.partial(gather_kernel, owners // 4, HEADS), out_...]
where the time goes in v3:
time: 70.4 us; the launch traced here: 70 us
  Pallas kernels  44.2 us (63%)
  local copies, waits for them, and re-layouts  17.3 us (25%)
  blocking collectives  3.56 us (5%)
  other arithmetic  2.74 us (4%)
  matrix products  1.26 us (2%)
  between operations  0.91 us (1%)
    pallas_call x1, Pallas kernels, gather_rows(): pl.pallas_call(functools.partial(gather_kernel, owners // 4, HEADS), out_...  37.4 us
    unnamed x32, local copies, waits for them, and re-layouts  14.3 us
    pallas_call x1, Pallas kernels, by_owner(): pl.pallas_call(functools.partial(decode_kernel, HEADS), out_shape=jax.Sha...  6.78 us
    psum x1, blocking collectives, by_owner(): totals = lax.psum(totals, 'grp')  3.56 us

profile of v3, /device:TPU:0, one launch (start us, length us, event | category | flops | bytes accessed | tf_op | source)
XLA Modules:
  0.0 70.0 jit_solution(10708563839175111185)
XLA Ops:
  0.6 0.0 copy-start
  0.6 0.0 copy-start.13
  0.7 1.0 %slice_reduce_fusion.2 = (s32[16,2,64]{2,1,0:T(2,128)S(1)}, s32[16,2,64]{2,1,0:T(2,128)S(1)}) fusion(s32[16,2,64,2]{2,3,1,0:T(2,128)} %param.17), kind=kLoop, calls=%fused_computation.35 | loop fusion | bytes 32768 | tf_op jit(solution)/shard_map/slice | solution.py:520
  1.7 0.1 reshape_squeeze.11
  1.8 0.1 reshape_squeeze.10
  1.9 0.7 fusion.13
  2.6 0.4 fusion
  3.1 0.1 select_reduce_fusion.1
  3.2 0.1 multiply_reduce_fusion
  3.4 0.8 %copy.52 = s32[16,2]{1,0:T(8,128)S(1)} copy(s32[16,2]{0,1:T(2,128)} %param.18) | data formatting | bytes 256 | tf_op args[8]
  4.1 0.1 lt.69
  4.2 0.1 lt.70
  4.3 0.1 lt.67
  4.4 0.1 compare_reduce_fusion
  4.5 0.2 convolution_convert_fusion.1
  4.7 0.4 select_reduce_fusion
  5.1 0.1 reshape.299
  5.2 0.5 broadcast_multiply_fusion.1
  5.7 0.0 copy-done
  5.7 0.0 copy-done.13
  5.7 0.7 convert_reduce_fusion
  6.4 0.2 fusion.4
  6.7 0.2 fusion.25
  6.9 0.0 copy-start.4
  6.9 0.2 fusion.5.normed_ref
  7.1 0.9 %pad.4.head_ref = bf16[32,768]{1,0:T(8,128)(2,1)S(1)} pad(bf16[28,768]{1,0:T(8,128)(2,1)} %bitcast.50, bf16[]{:T(256)} %constant.120.clone.1), padding=0_4x0_0 | pad | bytes 92162 | tf_op jit(solution)/shard_map/jit(_pad)/pad | solution.py:514
  8.0 0.2 copy-done.4
  8.3 1.3 %copy-done.5 = bf16[768,768]{1,0:T(8,128)(2,1)S(1)} copy-done((bf16[768,768]{1,0:T(8,128)(2,1)S(1)}, bf16[768,768]{1,0:T(8,128)(2,1)}, u32[]{:S(2)}) %copy-start.5) | copy-done | bytes 1179672
  9.5 37.4 %shard_map.113 = (bf16[512,8,768]{2,1,0:T(8,128)(2,1)S(1)}, f32[256,768]{1,0:T(8,128)S(1)}, bf16[384,768]{1,0:T(8,128)(2,1)S(1)}, f32[32,256]{1,0:T(8,128)S(1)}) custom-call(bf16[16,8,768]{2,1,0:T(8,128)(2,1)S(1)} %constant_dynamic-slice_fusion.own_ref, bf16[256,768]{1,0:T(8,128)(2,1)S(1)} %fusion.5.normed_ref, ...), custom_call_target="tpu_custom_call" | custom-call | tf_op jit(solution)/shard_map/pallas_call | solution.py:457
  47.0 2.7 %copy-done.1 = bf16[512,8,768]{2,1,0:T(8,128)(2,1)} copy-done((bf16[512,8,768]{2,1,0:T(8,128)(2,1)}, bf16[512,8,768]{2,1,0:T(8,128)(2,1)S(1)}, u32[]{:S(2)}) %copy-start.1) | copy-done | bytes 6291480
  49.6 0.9 %copy-done.7 = f32[256,768]{1,0:T(8,128)} copy-done((f32[256,768]{1,0:T(8,128)}, f32[256,768]{1,0:T(8,128)S(1)}, u32[]{:S(2)}) %copy-start.7) | copy-done | bytes 786456
  50.5 0.8 %copy-done.9 = bf16[384,768]{1,0:T(8,128)(2,1)} copy-done((bf16[384,768]{1,0:T(8,128)(2,1)}, bf16[384,768]{1,0:T(8,128)(2,1)S(1)}, u32[]{:S(2)}) %copy-start.9) | copy-done | bytes 589848
  51.3 0.1 iota_add_fusion
  51.4 0.1 add.134.place_ref
  51.5 0.0 copy-done.11
  51.5 0.1 broadcast_in_dim.30
  51.6 0.1 reshape.302.live_ref
  51.7 0.0 copy-start.2
  51.7 2.8 %copy-done.2 = bf16[512,8,768]{2,1,0:T(8,128)(2,1)S(1)} copy-done((bf16[512,8,768]{2,1,0:T(8,128)(2,1)S(1)}, bf16[512,8,768]{2,1,0:T(8,128)(2,1)}, u32[]{:S(2)}) %copy-start.2) | copy-done | bytes 6291480
  54.5 1.3 %copy-done.6 = bf16[768,768]{1,0:T(8,128)(2,1)S(1)} copy-done((bf16[768,768]{1,0:T(8,128)(2,1)S(1)}, bf16[768,768]{1,0:T(8,128)(2,1)}, u32[]{:S(2)}) %copy-start.6) | copy-done | bytes 1179672
  55.8 1.1 %copy-done.8 = f32[256,768]{1,0:T(8,128)S(1)} copy-done((f32[256,768]{1,0:T(8,128)S(1)}, f32[256,768]{1,0:T(8,128)}, u32[]{:S(2)}) %copy-start.8) | copy-done | bytes 786456
  56.9 1.1 %copy-done.10 = bf16[384,768]{1,0:T(8,128)(2,1)S(1)} copy-done((bf16[384,768]{1,0:T(8,128)(2,1)S(1)}, bf16[384,768]{1,0:T(8,128)(2,1)}, u32[]{:S(2)}) %copy-start.10) | copy-done | bytes 589848
  58.0 6.8 %shard_map.114 = f32[32,256]{1,0:T(8,128)S(1)} custom-call(s32[128]{0:T(128)S(1)} %get-tuple-element.35.source_ref, s32[128]{0:T(128)S(1)} %get-tuple-element.25.local_ref, bf16[512,8,768]{2,1,0:T(8,128)(2,1)S(1)} %copy-done.2, f32[256,768]{1,0:T(8,128)S(1)} %copy-done.8, bf16[768,768]{1,0:T(8,128)(2,1)S(1)} %copy-done.6, bf16[384,768]{1,0:T(8,128)(2,1)S(1)} %copy-done.10, ...), custom_call_target="tpu_custom_call" | custom-call | tf_op jit(solution)/shard_map/pallas_call | solution.py:550
  64.8 3.6 %psum.7 = f32[32,256]{1,0:T(8,128)S(1)} all-reduce(f32[32,256]{1,0:T(8,128)S(1)} %shard_map.114), channel_id=1, replica_groups=mesh['img'=16,'grp'=2] {'grp'}, use_global_device_ids=true, to_apply=%region_4.5 | all-reduce | flops 8192 | bytes 65536 | tf_op jit(solution)/shard_map/psum | solution.py:565
  68.3 0.1 copy.53
  68.5 0.1 copy.54
  68.6 0.7 copy.55
  69.3 0.7 copy.56
  (34 shorter events, 0.3 us)
Async XLA Ops:
  0.6 5.1 %copy-start = (bf16[1024,768]{1,0:T(8,128)(2,1)S(1)}, bf16[1024,768]{1,0:T(8,128)(2,1)}, u32[]{:S(2)}) copy-start(bf16[1024,768]{1,0:T(8,128)(2,1)} %param.11) | copy-start | bytes 4718596
  0.6 5.1 %copy-start.13 = (bf16[32,8,1024]{2,1,0:T(8,128)(2,1)S(1)}, bf16[32,8,1024]{2,1,0:T(8,128)(2,1)}, u32[]{:S(2)}) copy-start(bf16[32,8,1024]{2,1,0:T(8,128)(2,1)} %param.10) | copy-start | bytes 1572868
  6.4 1.6 %copy-start.3 = (bf16[768,768]{1,0:T(8,128)(2,1)S(1)}, bf16[768,768]{1,0:T(8,128)(2,1)}, u32[]{:S(2)}) copy-start(bf16[768,768]{1,0:T(8,128)(2,1)} %query_hbm.1) | copy-start | bytes 3538948
  6.9 1.4 %copy-start.4 = (bf16[768,768]{1,0:T(8,128)(2,1)S(1)}, bf16[768,768]{1,0:T(8,128)(2,1)}, u32[]{:S(2)}) copy-start(bf16[768,768]{1,0:T(8,128)(2,1)} %out_hbm.1) | copy-start | bytes 3538948
  8.3 1.3 %copy-start.5 = (bf16[768,768]{1,0:T(8,128)(2,1)S(1)}, bf16[768,768]{1,0:T(8,128)(2,1)}, u32[]{:S(2)}) copy-start(bf16[768,768]{1,0:T(8,128)(2,1)} %value_hbm.1) | copy-start | bytes 3538948
  9.5 41.8 %copy-start.12 = (s32[128]{0:T(128)S(1)}, s32[128]{0:T(128)}, u32[]{:S(2)}) copy-start(s32[128]{0:T(128)} %get-tuple-element.24) | copy-start | bytes 1540
  9.5 42.0 %copy-start.11 = (s32[128]{0:T(128)S(1)}, s32[128]{0:T(128)}, u32[]{:S(2)}) copy-start(s32[128]{0:T(128)} %get-tuple-element.34) | copy-start | bytes 1540
  47.0 2.7 %copy-start.1 = (bf16[512,8,768]{2,1,0:T(8,128)(2,1)}, bf16[512,8,768]{2,1,0:T(8,128)(2,1)S(1)}, u32[]{:S(2)}) copy-start(bf16[512,8,768]{2,1,0:T(8,128)(2,1)S(1)} %get-tuple-element.6.normed_ref) | copy-start | bytes 18874372
  49.6 0.9 %copy-start.7 = (f32[256,768]{1,0:T(8,128)}, f32[256,768]{1,0:T(8,128)S(1)}, u32[]{:S(2)}) copy-start(f32[256,768]{1,0:T(8,128)S(1)} %get-tuple-element.7.query_ref) | copy-start | bytes 2359300
  50.5 0.8 %copy-start.9 = (bf16[384,768]{1,0:T(8,128)(2,1)}, bf16[384,768]{1,0:T(8,128)(2,1)S(1)}, u32[]{:S(2)}) copy-start(bf16[384,768]{1,0:T(8,128)(2,1)S(1)} %get-tuple-element.8.value_ref) | copy-start | bytes 1769476
  51.7 2.8 %copy-start.2 = (bf16[512,8,768]{2,1,0:T(8,128)(2,1)S(1)}, bf16[512,8,768]{2,1,0:T(8,128)(2,1)}, u32[]{:S(2)}) copy-start(bf16[512,8,768]{2,1,0:T(8,128)(2,1)} %copy-done.1) | copy-start | bytes 18874372
  54.5 1.3 %copy-start.6 = (bf16[768,768]{1,0:T(8,128)(2,1)S(1)}, bf16[768,768]{1,0:T(8,128)(2,1)}, u32[]{:S(2)}) copy-start(bf16[768,768]{1,0:T(8,128)(2,1)} %key_ref.1) | copy-start | bytes 3538948
  55.8 1.1 %copy-start.8 = (f32[256,768]{1,0:T(8,128)S(1)}, f32[256,768]{1,0:T(8,128)}, u32[]{:S(2)}) copy-start(f32[256,768]{1,0:T(8,128)} %copy-done.7) | copy-start | bytes 2359300
  56.9 1.1 %copy-start.10 = (bf16[384,768]{1,0:T(8,128)(2,1)S(1)}, bf16[384,768]{1,0:T(8,128)(2,1)}, u32[]{:S(2)}) copy-start(bf16[384,768]{1,0:T(8,128)(2,1)} %copy-done.9) | copy-start | bytes 1769476

commit v4 on v3

--- a/solution.py
+++ b/solution.py
@@ -175,7 +175,7 @@
 NT = (((1,), (1,)), ((), ()))
 
 
-def decode_kernel(
+def decode(
     heads, source_ref, local_ref, normed_ref, query_ref, key_ref, value_ref, base_ref, place_ref,
     live_ref, out_ref, partner_rows, query_rows, attended
 ):
@@ -187,9 +187,8 @@
 
     def fetch(end, carry):
         at = pl.ds(pl.multiple_of(end * patches, patches), patches)
-        own = pl.ds(pl.multiple_of(local_ref[end] * patches, patches), patches)
         partner_rows[at, :] = normed_ref[source_ref[end]].astype(jnp.float32)
-        query_rows[at, :] = query_ref[own, :]
+        query_rows[at, :] = query_ref[local_ref[end]]
         return carry
 
     lax.fori_loop(0, ends, fetch, 0, unroll=8)
@@ -264,9 +263,10 @@
 
 
 def gather_kernel(
-    depth, heads, own_ref, normed_ref, embedded_ref, head_ref, query_hbm, out_hbm, value_hbm,
-    all_ref, query_ref, value_ref, base_ref, weights, weight_sem, place_sem, send_sem, recv_sem,
-    mate_send_sem, mate_recv_sem
+    depth, heads, source_ref, local_ref, place_ref, live_ref, own_ref, normed_ref, embedded_ref,
+    head_ref, query_hbm, out_hbm, value_hbm, key_hbm, totals_ref, all_ref, query_ref, value_ref,
+    base_ref, partner_rows, query_rows, attended, weights, weight_sem, place_sem, send_sem,
+    recv_sem, mate_send_sem, mate_recv_sem
 ):
     share = own_ref.shape[0]
     me = lax.axis_index("img")
@@ -277,7 +277,7 @@
     mesh_ids = pl.DeviceIdType.MESH
     loads = [
         pltpu.make_async_copy(source, weights.at[index], weight_sem.at[index])
-        for index, source in enumerate((query_hbm, out_hbm, value_hbm))
+        for index, source in enumerate((query_hbm, out_hbm, value_hbm, key_hbm))
     ]
     for load in loads:
         load.start()
@@ -286,7 +286,8 @@
         head_size = normed_ref.shape[1] // heads
         loads[0].wait()
         asked = jnp.dot(normed_ref[...], weights[0], preferred_element_type=jnp.float32)
-        query_ref[...] = asked.astype(jnp.bfloat16).astype(jnp.float32) / math.sqrt(head_size)
+        asked = asked.astype(jnp.bfloat16).astype(jnp.float32) / math.sqrt(head_size)
+        query_ref[...] = asked.reshape(query_ref.shape)
         base_ref[...] = lax.dot_general(
             head_ref[...], embedded_ref[...], NT, preferred_element_type=jnp.float32
         )
@@ -447,26 +448,38 @@
         return carry
 
     lax.fori_loop(0, 4 * depth, from_mate, 0)
-
-
-def gather_rows(outgoing, owners, normed, embedded, head_weight, w_query, w_out, w_value):
+    loads[3].wait()
+    decode(
+        heads, source_ref, local_ref, all_ref, query_ref, weights.at[3], value_ref, base_ref,
+        place_ref, live_ref, totals_ref, partner_rows, query_rows, attended
+    )
+
+
+def gather_and_decode(
+    owners, source, local, place, live_rows, outgoing, normed, embedded, head_weight, w_query,
+    w_out, w_value, w_key
+):
     share, patches, width = outgoing.shape
     wide = head_weight.shape[0]
+    rows = place.shape[1]
+    smem = pl.BlockSpec(memory_space=pltpu.SMEM)
     vmem = pl.BlockSpec(memory_space=pltpu.VMEM)
     away = pl.BlockSpec(memory_space=pl.ANY)
     return pl.pallas_call(
         functools.partial(gather_kernel, owners // 4, HEADS),
-        out_shape=(
-            jax.ShapeDtypeStruct((owners * 2 * share, patches, width), outgoing.dtype),
-            jax.ShapeDtypeStruct(normed.shape, jnp.float32),
-            jax.ShapeDtypeStruct((HEADS * wide, width), jnp.bfloat16),
-            jax.ShapeDtypeStruct((wide, normed.shape[0]), jnp.float32),
-        ),
-        in_specs=[vmem] * 4 + [away] * 3,
-        out_specs=(vmem,) * 4,
+        out_shape=jax.ShapeDtypeStruct((wide, normed.shape[0]), jnp.float32),
+        in_specs=[smem] * 2 + [vmem] * 6 + [away] * 4,
+        out_specs=vmem,
         scratch_shapes=[
-            pltpu.VMEM((3, width, width), jnp.bfloat16),
-            pltpu.SemaphoreType.DMA((3,)),
+            pltpu.VMEM((owners * 2 * share, patches, width), outgoing.dtype),
+            pltpu.VMEM((normed.shape[0] // patches, patches, width), jnp.float32),
+            pltpu.VMEM((HEADS * wide, width), jnp.bfloat16),
+            pltpu.VMEM((wide, normed.shape[0]), jnp.float32),
+            pltpu.VMEM((rows, width), jnp.float32),
+            pltpu.VMEM((rows, width), jnp.float32),
+            pltpu.VMEM((wide, rows), jnp.float32),
+            pltpu.VMEM((4, width, width), jnp.bfloat16),
+            pltpu.SemaphoreType.DMA((4,)),
             pltpu.SemaphoreType.DMA,
             pltpu.SemaphoreType.DMA((4, owners)),
             pltpu.SemaphoreType.DMA((owners,)),
@@ -474,9 +487,12 @@
             pltpu.SemaphoreType.DMA((owners,)),
         ],
         compiler_params=pltpu.CompilerParams(
-            collective_id=0, has_side_effects=True, vmem_limit_bytes=32 * 2**20
+            collective_id=0, has_side_effects=True, vmem_limit_bytes=48 * 2**20
         ),
-    )(outgoing, normed, embedded, head_weight, w_query, w_out, w_value)
+    )(
+        source, local, place, live_rows, outgoing, normed, embedded, head_weight, w_query, w_out,
+        w_value, w_key
+    )
 
 
 def look_up(owner_row, ids, img_dev):
@@ -512,9 +528,6 @@
     )
     wide = -(-channels // 8) * 8
     head_weight = jnp.pad(w_head.T, ((0, wide - channels), (0, 0)))
-    everyone, queries, value_head, base = gather_rows(
-        outgoing, owners, normed, embedded, head_weight, w_query, w_out, w_value
-    )
 
     end_count = groups * pair_cap * 2
     sides = [pair_images[..., s].reshape(owners, groups * pair_cap) for s in range(2)]
@@ -544,23 +557,9 @@
     place = chosen_local[:, None] * patches + jnp.arange(patches, dtype=jnp.int32)[None, :]
     live_rows = jnp.broadcast_to(chosen_live[:, None], (ends, patches)).reshape(1, -1)
 
-    smem = pl.BlockSpec(memory_space=pltpu.SMEM)
-    vmem = pl.BlockSpec(memory_space=pltpu.VMEM)
-    rows = ends * patches
-    totals = pl.pallas_call(
-        functools.partial(decode_kernel, HEADS),
-        out_shape=jax.ShapeDtypeStruct((wide, own_rows), jnp.float32),
-        in_specs=[smem, smem] + [vmem] * 7,
-        out_specs=vmem,
-        scratch_shapes=[
-            pltpu.VMEM((rows, dec_width), jnp.float32),
-            pltpu.VMEM((rows, dec_width), jnp.float32),
-            pltpu.VMEM((wide, rows), jnp.float32),
-        ],
-        compiler_params=pltpu.CompilerParams(vmem_limit_bytes=40 * 2**20),
-    )(
-        chosen_partner, chosen_local, everyone, queries, w_key, value_head, base,
-        place.reshape(1, -1), live_rows,
+    totals = gather_and_decode(
+        owners, chosen_partner, chosen_local, place.reshape(1, -1), live_rows, outgoing, normed,
+        embedded, head_weight, w_query, w_out, w_value, w_key
     )
     totals = lax.psum(totals, "grp")
     totals = totals[:channels].reshape(channels, img_dev, patches).transpose(1, 0, 2)

time: 70.4 us -> 59 us (0.84)
  local copies, waits for them, and re-layouts: 17.3 us -> 6.14 us
    unnamed x32 -> x16, local copies, waits for them, and re-layouts: 14.3 us -> 3.26 us
    pallas_call x2 -> x1, Pallas kernels: 44.2 us -> 44.5 us  [gather_and_decode(): pl.pallas_call(functools.partial(gather_kernel, owners // 4, HEADS), out_...]
where the time goes in v4:
time: 59 us; the launch traced here: 58.7 us
  Pallas kernels  44.5 us (75%)
  local copies, waits for them, and re-layouts  6.14 us (10%)
  blocking collectives  3.53 us (6%)
  other arithmetic  2.35 us (4%)
  matrix products  1.25 us (2%)
  between operations  0.91 us (2%)
    pallas_call x1, Pallas kernels, gather_and_decode(): pl.pallas_call(functools.partial(gather_kernel, owners // 4, HEADS), out_...  44.5 us
    psum x1, blocking collectives, by_owner(): totals = lax.psum(totals, 'grp')  3.53 us
    unnamed x16, local copies, waits for them, and re-layouts  3.26 us

profile of v4, /device:TPU:0, one launch (start us, length us, event | category | flops | bytes accessed | tf_op | source)
XLA Modules:
  0.0 58.7 jit_solution(10625715990937946544)
XLA Ops:
  0.6 0.0 copy-start
  0.6 0.0 copy-start.5
  0.7 0.1 lt.67
  0.8 0.8 %fusion.13 = (bf16[4,128]{1,0:T(4,128)(2,1)S(1)}, bf16[4,128]{1,0:T(4,128)(2,1)S(1)}) fusion(s32[512]{0:T(512)} %param.19), kind=kLoop, calls=%fused_computation.49 | loop fusion | flops 10752 | bytes 4096 | tf_op jit(solution)/shard_map/convert.1
  1.6 0.8 %copy.52 = s32[16,2]{1,0:T(8,128)S(1)} copy(s32[16,2]{0,1:T(2,128)} %param.18) | data formatting | bytes 256 | tf_op args[8]
  2.3 0.1 lt.69
  2.4 0.1 lt.70
  2.5 0.9 %slice_reduce_fusion.2 = (s32[16,2,64]{2,1,0:T(2,128)S(1)}, s32[16,2,64]{2,1,0:T(2,128)S(1)}) fusion(s32[16,2,64,2]{2,3,1,0:T(2,128)} %param.17), kind=kLoop, calls=%fused_computation.35 | loop fusion | bytes 32768 | tf_op jit(solution)/shard_map/slice | solution.py:533
  3.5 0.1 reshape_squeeze.10
  3.5 0.1 reshape_squeeze.11
  3.7 0.8 %pad.4.head_ref = bf16[32,768]{1,0:T(8,128)(2,1)S(1)} pad(bf16[28,768]{1,0:T(8,128)(2,1)} %bitcast.50, bf16[]{:T(256)} %constant.120.clone.1), padding=0_4x0_0 | pad | bytes 92162 | tf_op jit(solution)/shard_map/jit(_pad)/pad | solution.py:530
  4.5 0.4 fusion
  5.0 0.1 select_reduce_fusion.1
  5.1 0.1 compare_reduce_fusion
  5.2 0.1 multiply_reduce_fusion
  5.4 0.2 convolution_convert_fusion.1
  5.5 0.4 select_reduce_fusion
  5.9 0.1 reshape.299
  6.1 0.1 iota_add_fusion
  6.1 0.1 add.131.place_ref
  6.2 0.1 broadcast_in_dim.30
  6.3 0.1 reshape.300.live_ref
  6.4 0.0 copy-done
  6.4 0.0 copy-done.5
  6.4 0.0 copy-start.3
  6.5 0.0 copy-start.4
  6.5 0.7 %convert_reduce_fusion = (f32[256]{0:T(256)S(1)}, bf16[256,768]{1,0:T(8,128)(2,1)S(1)}) fusion(bf16[1024,768]{1,0:T(8,128)(2,1)S(1)} %copy-done, bf16[32,8,1024]{2,1,0:T(8,128)(2,1)S(1)} %copy-done.5), kind=kOutput, calls=%fused_computation.6 | convolution fusion | flops 403242752 | bytes 2491392 | tf_op jit(solution)/shard_map/dot_general | solution.py:522
  7.1 0.0 copy-start.1
  7.1 0.0 copy-start.2
  7.2 0.2 fusion.4
  7.4 0.2 fusion.25
  7.7 0.2 fusion.5.normed_ref
  7.9 0.0 copy-done.3
  7.9 0.2 copy-done.4
  8.1 0.5 copy-done.1
  8.6 0.4 copy-done.2
  9.0 44.5 %shard_map.113 = f32[32,256]{1,0:T(8,128)S(1)} custom-call(s32[128]{0:T(128)S(1)} %get-tuple-element.27.source_ref, s32[128]{0:T(128)S(1)} %get-tuple-element.17.local_ref, s32[1,1024]{1,0:T(1,128)S(1)} %add.131.place_ref, s32[1,1024]{1,0:T(1,128)S(1)} %reshape.300.live_ref, bf16[16,8,768]{2,1,0:T(8,128)(2,1)S(1)} %constant_dynamic-slice_fusion.own_ref, ...), custom_call_target="tpu_custom_call" | custom-call | tf_op jit(solution)/shard_map/pallas_call | solution.py:468
  53.4 3.5 %psum.7 = f32[32,256]{1,0:T(8,128)S(1)} all-reduce(f32[32,256]{1,0:T(8,128)S(1)} %shard_map.113), channel_id=1, replica_groups=mesh['img'=16,'grp'=2] {'grp'}, use_global_device_ids=true, to_apply=%region_4.5 | all-reduce | flops 8192 | bytes 65536 | tf_op jit(solution)/shard_map/psum | solution.py:564
  57.0 0.1 copy.53
  57.1 0.1 copy.54
  57.3 0.7 %copy.56 = f32[32,192]{1,0:T(8,128)} copy(f32[32,192]{0,1:T(8,128)S(1)} %fusion.7) | data formatting | bytes 49152
  58.0 0.7 %copy.55 = f32[32,32]{1,0:T(8,128)} copy(f32[32,32]{0,1:T(8,128)S(1)} %maximum_bitcast_fusion) | data formatting | bytes 8192
  (23 shorter events, 0.3 us)
Async XLA Ops:
  0.6 5.8 %copy-start = (bf16[1024,768]{1,0:T(8,128)(2,1)S(1)}, bf16[1024,768]{1,0:T(8,128)(2,1)}, u32[]{:S(2)}) copy-start(bf16[1024,768]{1,0:T(8,128)(2,1)} %param.11) | copy-start | bytes 4718596
  0.6 5.8 %copy-start.5 = (bf16[32,8,1024]{2,1,0:T(8,128)(2,1)S(1)}, bf16[32,8,1024]{2,1,0:T(8,128)(2,1)}, u32[]{:S(2)}) copy-start(bf16[32,8,1024]{2,1,0:T(8,128)(2,1)} %param.10) | copy-start | bytes 1572868
  6.4 1.4 %copy-start.3 = (bf16[768,768]{1,0:T(8,128)(2,1)S(1)}, bf16[768,768]{1,0:T(8,128)(2,1)}, u32[]{:S(2)}) copy-start(bf16[768,768]{1,0:T(8,128)(2,1)} %value_hbm.1) | copy-start | bytes 3538948
  6.5 1.6 %copy-start.4 = (bf16[768,768]{1,0:T(8,128)(2,1)S(1)}, bf16[768,768]{1,0:T(8,128)(2,1)}, u32[]{:S(2)}) copy-start(bf16[768,768]{1,0:T(8,128)(2,1)} %key_hbm.1) | copy-start | bytes 3538948
  7.1 1.5 %copy-start.1 = (bf16[768,768]{1,0:T(8,128)(2,1)S(1)}, bf16[768,768]{1,0:T(8,128)(2,1)}, u32[]{:S(2)}) copy-start(bf16[768,768]{1,0:T(8,128)(2,1)} %query_hbm.1) | copy-start | bytes 3538948
  7.1 1.8 %copy-start.2 = (bf16[768,768]{1,0:T(8,128)(2,1)S(1)}, bf16[768,768]{1,0:T(8,128)(2,1)}, u32[]{:S(2)}) copy-start(bf16[768,768]{1,0:T(8,128)(2,1)} %out_hbm.1) | copy-start | bytes 3538948

commit v5 on v4

--- a/solution.py
+++ b/solution.py
@@ -188,7 +188,6 @@
     def fetch(end, carry):
         at = pl.ds(pl.multiple_of(end * patches, patches), patches)
         partner_rows[at, :] = normed_ref[source_ref[end]].astype(jnp.float32)
-        query_rows[at, :] = query_ref[local_ref[end]]
         return carry
 
     lax.fori_loop(0, ends, fetch, 0, unroll=8)
@@ -292,6 +291,16 @@
             head_ref[...], embedded_ref[...], NT, preferred_element_type=jnp.float32
         )
 
+    def place_queries():
+        patches = query_ref.shape[1]
+
+        def fetch(end, carry):
+            at = pl.ds(pl.multiple_of(end * patches, patches), patches)
+            query_rows[at, :] = query_ref[local_ref[end]]
+            return carry
+
+        lax.fori_loop(0, local_ref.shape[0], fetch, 0, unroll=8)
+
     def value_to_head():
         head_size = normed_ref.shape[1] // heads
         channels = head_ref.shape[0]
@@ -431,7 +440,7 @@
 
     place = pltpu.make_async_copy(own_ref, slot(me), place_sem)
     place.start()
-    run(begin, {0: own_queries, 1: value_to_head})
+    run(begin, {0: own_queries, 1: value_to_head, 2: place_queries})
     run(finish, {})
     place.wait()
 

time: 59 us -> 58.7 us (level)
  no operation moved by 1% of the time
where the time goes in v5:
time: 58.7 us; the launch traced here: 58.4 us
  Pallas kernels  44.2 us (75%)
  local copies, waits for them, and re-layouts  6.14 us (10%)
  blocking collectives  3.53 us (6%)
  other arithmetic  2.35 us (4%)
  matrix products  1.25 us (2%)
  between operations  0.91 us (2%)
    pallas_call x1, Pallas kernels, gather_and_decode(): pl.pallas_call(functools.partial(gather_kernel, owners // 4, HEADS), out_...  44.2 us
    psum x1, blocking collectives, by_owner(): totals = lax.psum(totals, 'grp')  3.53 us
    unnamed x16, local copies, waits for them, and re-layouts  3.26 us

profile of v5, /device:TPU:0, one launch (start us, length us, event | category | flops | bytes accessed | tf_op | source)
XLA Modules:
  0.0 58.4 jit_solution(2389322592220013203)
XLA Ops:
  0.6 0.0 copy-start
  0.6 0.0 copy-start.5
  0.7 0.1 lt.67
  0.8 0.8 %fusion.13 = (bf16[4,128]{1,0:T(4,128)(2,1)S(1)}, bf16[4,128]{1,0:T(4,128)(2,1)S(1)}) fusion(s32[512]{0:T(512)} %param.19), kind=kLoop, calls=%fused_computation.49 | loop fusion | flops 10752 | bytes 4096 | tf_op jit(solution)/shard_map/convert.1
  1.6 0.8 %copy.52 = s32[16,2]{1,0:T(8,128)S(1)} copy(s32[16,2]{0,1:T(2,128)} %param.18) | data formatting | bytes 256 | tf_op args[8]
  2.3 0.1 lt.69
  2.4 0.1 lt.70
  2.5 0.9 %slice_reduce_fusion.2 = (s32[16,2,64]{2,1,0:T(2,128)S(1)}, s32[16,2,64]{2,1,0:T(2,128)S(1)}) fusion(s32[16,2,64,2]{2,3,1,0:T(2,128)} %param.17), kind=kLoop, calls=%fused_computation.35 | loop fusion | bytes 32768 | tf_op jit(solution)/shard_map/slice | solution.py:542
  3.5 0.1 reshape_squeeze.10
  3.5 0.1 reshape_squeeze.11
  3.7 0.8 %pad.4.head_ref = bf16[32,768]{1,0:T(8,128)(2,1)S(1)} pad(bf16[28,768]{1,0:T(8,128)(2,1)} %bitcast.50, bf16[]{:T(256)} %constant.120.clone.1), padding=0_4x0_0 | pad | bytes 92162 | tf_op jit(solution)/shard_map/jit(_pad)/pad | solution.py:539
  4.5 0.4 fusion
  5.0 0.1 select_reduce_fusion.1
  5.1 0.1 compare_reduce_fusion
  5.2 0.1 multiply_reduce_fusion
  5.4 0.2 convolution_convert_fusion.1
  5.5 0.4 select_reduce_fusion
  5.9 0.1 reshape.299
  6.1 0.1 iota_add_fusion
  6.1 0.1 add.131.place_ref
  6.2 0.1 broadcast_in_dim.30
  6.3 0.1 reshape.300.live_ref
  6.4 0.0 copy-done
  6.4 0.0 copy-done.5
  6.4 0.0 copy-start.3
  6.5 0.0 copy-start.4
  6.5 0.7 %convert_reduce_fusion = (f32[256]{0:T(256)S(1)}, bf16[256,768]{1,0:T(8,128)(2,1)S(1)}) fusion(bf16[1024,768]{1,0:T(8,128)(2,1)S(1)} %copy-done, bf16[32,8,1024]{2,1,0:T(8,128)(2,1)S(1)} %copy-done.5), kind=kOutput, calls=%fused_computation.6 | convolution fusion | flops 403242752 | bytes 2491392 | tf_op jit(solution)/shard_map/dot_general | solution.py:531
  7.1 0.0 copy-start.1
  7.1 0.0 copy-start.2
  7.2 0.2 fusion.4
  7.4 0.2 fusion.25
  7.7 0.2 fusion.5.normed_ref
  7.9 0.0 copy-done.3
  7.9 0.2 copy-done.4
  8.1 0.5 copy-done.1
  8.6 0.4 copy-done.2
  9.0 44.2 %shard_map.113 = f32[32,256]{1,0:T(8,128)S(1)} custom-call(s32[128]{0:T(128)S(1)} %get-tuple-element.27.source_ref, s32[128]{0:T(128)S(1)} %get-tuple-element.17.local_ref, s32[1,1024]{1,0:T(1,128)S(1)} %add.131.place_ref, s32[1,1024]{1,0:T(1,128)S(1)} %reshape.300.live_ref, bf16[16,8,768]{2,1,0:T(8,128)(2,1)S(1)} %constant_dynamic-slice_fusion.own_ref, ...), custom_call_target="tpu_custom_call" | custom-call | tf_op jit(solution)/shard_map/pallas_call | solution.py:477
  53.1 3.5 %psum.7 = f32[32,256]{1,0:T(8,128)S(1)} all-reduce(f32[32,256]{1,0:T(8,128)S(1)} %shard_map.113), channel_id=1, replica_groups=mesh['img'=16,'grp'=2] {'grp'}, use_global_device_ids=true, to_apply=%region_4.5 | all-reduce | flops 8192 | bytes 65536 | tf_op jit(solution)/shard_map/psum | solution.py:573
  56.7 0.1 copy.53
  56.8 0.1 copy.54
  57.0 0.7 %copy.56 = f32[32,192]{1,0:T(8,128)} copy(f32[32,192]{0,1:T(8,128)S(1)} %fusion.7) | data formatting | bytes 49152
  57.7 0.7 %copy.55 = f32[32,32]{1,0:T(8,128)} copy(f32[32,32]{0,1:T(8,128)S(1)} %maximum_bitcast_fusion) | data formatting | bytes 8192
  (23 shorter events, 0.3 us)
Async XLA Ops:
  0.6 5.8 %copy-start = (bf16[1024,768]{1,0:T(8,128)(2,1)S(1)}, bf16[1024,768]{1,0:T(8,128)(2,1)}, u32[]{:S(2)}) copy-start(bf16[1024,768]{1,0:T(8,128)(2,1)} %param.11) | copy-start | bytes 4718596
  0.6 5.8 %copy-start.5 = (bf16[32,8,1024]{2,1,0:T(8,128)(2,1)S(1)}, bf16[32,8,1024]{2,1,0:T(8,128)(2,1)}, u32[]{:S(2)}) copy-start(bf16[32,8,1024]{2,1,0:T(8,128)(2,1)} %param.10) | copy-start | bytes 1572868
  6.4 1.4 %copy-start.3 = (bf16[768,768]{1,0:T(8,128)(2,1)S(1)}, bf16[768,768]{1,0:T(8,128)(2,1)}, u32[]{:S(2)}) copy-start(bf16[768,768]{1,0:T(8,128)(2,1)} %value_hbm.1) | copy-start | bytes 3538948
  6.5 1.6 %copy-start.4 = (bf16[768,768]{1,0:T(8,128)(2,1)S(1)}, bf16[768,768]{1,0:T(8,128)(2,1)}, u32[]{:S(2)}) copy-start(bf16[768,768]{1,0:T(8,128)(2,1)} %key_hbm.1) | copy-start | bytes 3538948
  7.1 1.5 %copy-start.1 = (bf16[768,768]{1,0:T(8,128)(2,1)S(1)}, bf16[768,768]{1,0:T(8,128)(2,1)}, u32[]{:S(2)}) copy-start(bf16[768,768]{1,0:T(8,128)(2,1)} %query_hbm.1) | copy-start | bytes 3538948
  7.1 1.8 %copy-start.2 = (bf16[768,768]{1,0:T(8,128)(2,1)S(1)}, bf16[768,768]{1,0:T(8,128)(2,1)}, u32[]{:S(2)}) copy-start(bf16[768,768]{1,0:T(8,128)(2,1)} %out_hbm.1) | copy-start | bytes 3538948
